TPU v7x, 32 devices: a whole 2x2x4 slice. The times are simulated.
32 devices in a mesh: sta: 4 (over z), grp: 2 (over y), hr: 4 (over x, core).
Axes of the slice: x: 2, y: 2, z: 4, core: 2. Of those that a mesh axis runs over, the one named last changes fastest.
Arguments:
- spectra: bfloat16 [4, 32, 6, 8192], P('hr', 'sta'), may hold values from -6 to 6
- pair_source: int32 [128], P(('sta', 'grp')), may hold values from 0 to 7
- pair_owner: int32 [128, 1], P(('sta', 'grp')), may hold values from 0 to 3; in each aligned block of 16 rows (0 to 15, 16 to 31, ...) at most 8 rows name the same one
- pair_row: int32 [128], P(('sta', 'grp')), may hold values from 0 to 7
Outputs:
- stacked: float32 [128, 9, 1024], P(('sta', 'grp'))
Inputs may be any that keep to these rules, and one draw needn't show every extreme that they name: `pair_owner`: in each aligned block of 16 pairs (the pairs of one device) no value is named by more than 8 pairs, and in some block one value is named by exactly 8 pairs.
All inputs are finite; a program needn't handle non-finite values.
Results may differ from a plain program's by a relative error of at most 0.0032.
Values may be sent and summed in bfloat16 or wider, within the bound.
A program may use at most 128 MiB of HBM per device.

v0:
```python
import math

import jax
import jax.numpy as jnp
from jax import lax
from jax.sharding import PartitionSpec as P

LAGS = 1024


two_pi = 2.0 * math.pi


def lag_table(start_bin, block_size, num_bins):
    bin_index = start_bin + jnp.arange(block_size, dtype=jnp.int32)
    lag_shift = jnp.arange(LAGS, dtype=jnp.int32) - LAGS // 2
    period = 2 * num_bins
    angles = jnp.mod(bin_index[:, None] * lag_shift[None, :], period).astype(jnp.float32) * (
        two_pi / period
    )
    return jnp.concatenate([jnp.cos(angles), -jnp.sin(angles)], axis=0).astype(jnp.bfloat16)


def cross_block(src_blk, rcv_blk):
    source_part = src_blk.astype(jnp.float32)
    recv_part = rcv_blk.astype(jnp.float32)
    src_re = source_part[..., 0:3, :][..., :, None, :]
    src_im = source_part[..., 3:6, :][..., :, None, :]
    rcv_re = recv_part[..., 0:3, :][..., None, :, :]
    rcv_im = recv_part[..., 3:6, :][..., None, :, :]
    cross_re = src_re * rcv_re + src_im * rcv_im
    cross_im = src_re * rcv_im - src_im * rcv_re
    return jnp.concatenate([cross_re, cross_im], axis=-1).astype(jnp.bfloat16)


def window_taper():
    lag_pos = jnp.arange(LAGS, dtype=jnp.float32)
    return 0.75 - 0.25 * jnp.cos(two_pi * (lag_pos + 0.5) / LAGS)


def slot_layout(owners, pair_row, peer_count, slot_cap):
    onehot = (owners[:, None] == jnp.arange(peer_count, dtype=jnp.int32)[None, :]).astype(jnp.int32)
    before = jnp.cumsum(onehot, axis=0) - onehot
    slot_rank = jnp.sum(before * onehot, axis=1)
    slot_index = owners * slot_cap + slot_rank
    request_table = jnp.zeros((peer_count * slot_cap,), jnp.int32).at[slot_index].set(pair_row)
    return (slot_index, request_table)


def body(spectra, pair_source, pair_owner, pair_row):
    hours_dev, sta_dev, comp_rows, num_bins = spectra.shape
    pair_count = pair_source.shape[0]
    owners = pair_owner[:, 0]
    peer_count = lax.axis_size("sta")
    slot_cap = 2 * pair_count // peer_count
    slot_index, request_table = slot_layout(owners, pair_row, peer_count, slot_cap)
    slot_owner = jnp.arange(peer_count * slot_cap, dtype=jnp.int32) // slot_cap
    wanted_station = slot_owner * sta_dev + request_table
    picked = jnp.take(lax.all_gather(spectra, "sta", axis=1, tiled=True), wanted_station, axis=1)
    receivers = jnp.take(picked, slot_index, axis=1)
    sources = jnp.take(spectra, pair_source, axis=1)
    block_size = min(512, num_bins)
    row_count = hours_dev * pair_count * 9

    def add_block(block_index, running):
        start_bin = (block_index * block_size).astype(jnp.int32)
        src_blk = lax.dynamic_slice_in_dim(sources, start_bin, block_size, 3)
        rcv_blk = lax.dynamic_slice_in_dim(receivers, start_bin, block_size, 3)
        cross = cross_block(src_blk, rcv_blk).reshape(row_count, 2 * block_size)
        table = lag_table(start_bin, block_size, num_bins)
        return running + jnp.dot(cross, table, preferred_element_type=jnp.float32)

    running = lax.fori_loop(
        0, num_bins // block_size, add_block, jnp.zeros((row_count, LAGS), jnp.float32)
    )
    local_sum = jnp.sum(running.reshape(hours_dev, pair_count, 9, LAGS), axis=0)
    stacked_sum = lax.psum(local_sum, "hr")
    hour_total = hours_dev * lax.axis_size("hr")
    return stacked_sum * window_taper()[None, None, :] / (hour_total * math.sqrt(num_bins))


def solution(mesh):
    placed = (
        P("hr", "sta", None, None),
        P(("sta", "grp")),
        P(("sta", "grp"), None),
        P(("sta", "grp")),
    )
    return jax.shard_map(
        body, mesh=mesh, in_specs=placed, out_specs=P(("sta", "grp"), None, None), check_vma=False
    )
```

profile of v0, /device:TPU:1, one launch (start us, length us, event | category | flops | bytes accessed | tf_op | source)
XLA Modules:
  0.0 320.1 jit_solution(2618237629961703412)
XLA Ops:
  7.3 1.6 copy.17
  10.8 63.7 %all-gather.2.cloned.1.call-done = bf16[1,32,6,8192]{3,1,2,0:T(8,128)(2,1)} async-done(((bf16[1,8,6,8192]{3,1,2,0:T(8,128)(2,1)}), bf16[1,32,6,8192]{3,1,2,0:T(8,128)(2,1)}) %all-gather.2.cloned.1.call-update) | async-done | bytes 3145744 | tf_op jit(solution)/shard_map/all_gather | solution.py:59
  74.5 5.6 %copy.16 = bf16[1,32,6,8192]{3,2,1,0:T(8,128)(2,1)} copy(bf16[1,32,6,8192]{3,1,2,0:T(8,128)(2,1)} %all-gather.2.cloned.1.call-done) | data formatting | bytes 6291456 | tf_op jit(solution)/shard_map/all_gather | solution.py:59
  80.1 5.0 %gather_fusion.1 = bf16[32,6,8192]{2,1,0:T(8,128)(2,1)} fusion(bf16[32,6,8192]{2,1,0:T(8,128)(2,1)} %bitcast.37, s32[1024]{0:T(1024)S(1)} %pad_clamp_fusion.1), kind=kCustom, calls=%fused_computation.1 | custom fusion | bytes 6291584 | tf_op jit(solution)/shard_map/jit(_take)/gather | solution.py:59
  85.1 4.8 %fusion.14 = bf16[32,6,8192]{2,1,0:T(8,128)(2,1)} fusion(bf16[32,6,8192]{2,1,0:T(8,128)(2,1)} %gather_fusion.1, pred[32]{0:T(512)(128)(4,1)S(1)} %get-tuple-element.143), kind=kLoop, calls=%fused_computation.34 | loop fusion | flops 1572864 | bytes 6291488 | tf_op jit(solution)/shard_map/jit(_take)/select_n | solution.py:59
  89.8 4.2 %gather_fusion.2 = bf16[16,6,8192]{2,1,0:T(8,128)(2,1)} fusion(bf16[32,6,8192]{2,1,0:T(8,128)(2,1)} %fusion.14, s32[1024]{0:T(1024)S(1)} %pad_clamp_fusion), kind=kCustom, calls=%fused_computation.2 | custom fusion | bytes 3145792 | tf_op jit(solution)/shard_map/jit(_take)/gather | solution.py:60
  94.0 4.2 %bitcast_select_fusion.1 = (bf16[1,16,6,8192]{3,2,1,0:T(8,128)(2,1)}, bf16[1,16,6,8192]{3,2,1,0:T(8,128)(2,1)}) fusion(bf16[16,6,8192]{2,1,0:T(8,128)(2,1)} %gather_fusion.2, pred[16]{0:T(512)(128)(4,1)S(1)} %get-tuple-element.141, bf16[16,6,8192]{2,1,0:T(8,128)(2,1)S(1)} %gather_fusion, pred[16]{0:T(512)(128)(4,1)S(1)} %compare_and_fusion.1), kind=kLoop, calls=%fused_computation.36 | loop fusion | flops 1572864 | bytes 6291488 | tf_op jit(solution)/shard_map/jit(_take)/select_n | solution.py:60
  98.2 180.9 %while.16 = (s32[]{:T(128)}, f32[144,1024]{1,0:T(8,128)S(1)}, bf16[1,16,6,8192]{3,2,1,0:T(8,128)(2,1)}, bf16[1,16,6,8192]{3,2,1,0:T(8,128)(2,1)}, s32[]{:T(128)}, /*index=5*/s32[]{:T(128)}, s32[]{:T(128)}, s32[]{:T(128)}) while((s32[]{:T(128)}, f32[144,1024]{1,0:T(8,128)S(1)}, bf16[1,16,6,8192]{3,2,1,0:T(8,128)(2,1)}, ...), condition=%wide.region_4.5_spmd.clone, body=%wide.region_3.4_spmd.clone.sunk | while | flops 316671488 | bytes 8335509 | solution.py:73
  99.9 9.0 %cosine_convert_fusion.2 = (bf16[512,1024]{1,0:T(8,128)(2,1)S(1)}, bf16[512,1024]{1,0:T(8,128)(2,1)S(1)}) fusion(s32[1024]{0:T(1024)S(1)} %iota_add_fusion.4, s32[512]{0:T(512)S(1)} %iota_add_fusion.5), kind=kLoop, calls=%fused_computation.17.clone.1 | loop fusion | flops 8912896 | bytes 2103296 | tf_op jit(solution)/shard_map/convert
  109.6 1.0 dynamic-slice_convert_fusion.3
  111.2 9.0 %cosine_convert_fusion.2 = (bf16[512,1024]{1,0:T(8,128)(2,1)S(1)}, bf16[512,1024]{1,0:T(8,128)(2,1)S(1)}) fusion(s32[1024]{0:T(1024)S(1)} %iota_add_fusion.4, s32[512]{0:T(512)S(1)} %iota_add_fusion.5), kind=kLoop, calls=%fused_computation.17.clone.1 | loop fusion | flops 8912896 | bytes 2103296 | tf_op jit(solution)/shard_map/convert
  120.9 1.0 dynamic-slice_convert_fusion.3
  122.5 9.0 %cosine_convert_fusion.2 = (bf16[512,1024]{1,0:T(8,128)(2,1)S(1)}, bf16[512,1024]{1,0:T(8,128)(2,1)S(1)}) fusion(s32[1024]{0:T(1024)S(1)} %iota_add_fusion.4, s32[512]{0:T(512)S(1)} %iota_add_fusion.5), kind=kLoop, calls=%fused_computation.17.clone.1 | loop fusion | flops 8912896 | bytes 2103296 | tf_op jit(solution)/shard_map/convert
  132.2 1.0 dynamic-slice_convert_fusion.3
  133.8 9.0 %cosine_convert_fusion.2 = (bf16[512,1024]{1,0:T(8,128)(2,1)S(1)}, bf16[512,1024]{1,0:T(8,128)(2,1)S(1)}) fusion(s32[1024]{0:T(1024)S(1)} %iota_add_fusion.4, s32[512]{0:T(512)S(1)} %iota_add_fusion.5), kind=kLoop, calls=%fused_computation.17.clone.1 | loop fusion | flops 8912896 | bytes 2103296 | tf_op jit(solution)/shard_map/convert
  143.5 1.0 dynamic-slice_convert_fusion.3
  145.1 9.0 %cosine_convert_fusion.2 = (bf16[512,1024]{1,0:T(8,128)(2,1)S(1)}, bf16[512,1024]{1,0:T(8,128)(2,1)S(1)}) fusion(s32[1024]{0:T(1024)S(1)} %iota_add_fusion.4, s32[512]{0:T(512)S(1)} %iota_add_fusion.5), kind=kLoop, calls=%fused_computation.17.clone.1 | loop fusion | flops 8912896 | bytes 2103296 | tf_op jit(solution)/shard_map/convert
  156.4 9.0 %cosine_convert_fusion.2 = (bf16[512,1024]{1,0:T(8,128)(2,1)S(1)}, bf16[512,1024]{1,0:T(8,128)(2,1)S(1)}) fusion(s32[1024]{0:T(1024)S(1)} %iota_add_fusion.4, s32[512]{0:T(512)S(1)} %iota_add_fusion.5), kind=kLoop, calls=%fused_computation.17.clone.1 | loop fusion | flops 8912896 | bytes 2103296 | tf_op jit(solution)/shard_map/convert
  167.7 9.0 %cosine_convert_fusion.2 = (bf16[512,1024]{1,0:T(8,128)(2,1)S(1)}, bf16[512,1024]{1,0:T(8,128)(2,1)S(1)}) fusion(s32[1024]{0:T(1024)S(1)} %iota_add_fusion.4, s32[512]{0:T(512)S(1)} %iota_add_fusion.5), kind=kLoop, calls=%fused_computation.17.clone.1 | loop fusion | flops 8912896 | bytes 2103296 | tf_op jit(solution)/shard_map/convert
  179.1 9.0 %cosine_convert_fusion.2 = (bf16[512,1024]{1,0:T(8,128)(2,1)S(1)}, bf16[512,1024]{1,0:T(8,128)(2,1)S(1)}) fusion(s32[1024]{0:T(1024)S(1)} %iota_add_fusion.4, s32[512]{0:T(512)S(1)} %iota_add_fusion.5), kind=kLoop, calls=%fused_computation.17.clone.1 | loop fusion | flops 8912896 | bytes 2103296 | tf_op jit(solution)/shard_map/convert
  190.4 9.0 %cosine_convert_fusion.2 = (bf16[512,1024]{1,0:T(8,128)(2,1)S(1)}, bf16[512,1024]{1,0:T(8,128)(2,1)S(1)}) fusion(s32[1024]{0:T(1024)S(1)} %iota_add_fusion.4, s32[512]{0:T(512)S(1)} %iota_add_fusion.5), kind=kLoop, calls=%fused_computation.17.clone.1 | loop fusion | flops 8912896 | bytes 2103296 | tf_op jit(solution)/shard_map/convert
  201.7 9.0 %cosine_convert_fusion.2 = (bf16[512,1024]{1,0:T(8,128)(2,1)S(1)}, bf16[512,1024]{1,0:T(8,128)(2,1)S(1)}) fusion(s32[1024]{0:T(1024)S(1)} %iota_add_fusion.4, s32[512]{0:T(512)S(1)} %iota_add_fusion.5), kind=kLoop, calls=%fused_computation.17.clone.1 | loop fusion | flops 8912896 | bytes 2103296 | tf_op jit(solution)/shard_map/convert
  213.0 9.0 %cosine_convert_fusion.2 = (bf16[512,1024]{1,0:T(8,128)(2,1)S(1)}, bf16[512,1024]{1,0:T(8,128)(2,1)S(1)}) fusion(s32[1024]{0:T(1024)S(1)} %iota_add_fusion.4, s32[512]{0:T(512)S(1)} %iota_add_fusion.5), kind=kLoop, calls=%fused_computation.17.clone.1 | loop fusion | flops 8912896 | bytes 2103296 | tf_op jit(solution)/shard_map/convert
  224.3 9.0 %cosine_convert_fusion.2 = (bf16[512,1024]{1,0:T(8,128)(2,1)S(1)}, bf16[512,1024]{1,0:T(8,128)(2,1)S(1)}) fusion(s32[1024]{0:T(1024)S(1)} %iota_add_fusion.4, s32[512]{0:T(512)S(1)} %iota_add_fusion.5), kind=kLoop, calls=%fused_computation.17.clone.1 | loop fusion | flops 8912896 | bytes 2103296 | tf_op jit(solution)/shard_map/convert
  235.6 9.0 %cosine_convert_fusion.2 = (bf16[512,1024]{1,0:T(8,128)(2,1)S(1)}, bf16[512,1024]{1,0:T(8,128)(2,1)S(1)}) fusion(s32[1024]{0:T(1024)S(1)} %iota_add_fusion.4, s32[512]{0:T(512)S(1)} %iota_add_fusion.5), kind=kLoop, calls=%fused_computation.17.clone.1 | loop fusion | flops 8912896 | bytes 2103296 | tf_op jit(solution)/shard_map/convert
  245.2 1.0 dynamic-slice_convert_fusion.3
  246.9 9.0 %cosine_convert_fusion.2 = (bf16[512,1024]{1,0:T(8,128)(2,1)S(1)}, bf16[512,1024]{1,0:T(8,128)(2,1)S(1)}) fusion(s32[1024]{0:T(1024)S(1)} %iota_add_fusion.4, s32[512]{0:T(512)S(1)} %iota_add_fusion.5), kind=kLoop, calls=%fused_computation.17.clone.1 | loop fusion | flops 8912896 | bytes 2103296 | tf_op jit(solution)/shard_map/convert
  258.2 9.0 %cosine_convert_fusion.2 = (bf16[512,1024]{1,0:T(8,128)(2,1)S(1)}, bf16[512,1024]{1,0:T(8,128)(2,1)S(1)}) fusion(s32[1024]{0:T(1024)S(1)} %iota_add_fusion.4, s32[512]{0:T(512)S(1)} %iota_add_fusion.5), kind=kLoop, calls=%fused_computation.17.clone.1 | loop fusion | flops 8912896 | bytes 2103296 | tf_op jit(solution)/shard_map/convert
  269.5 9.0 %cosine_convert_fusion.2 = (bf16[512,1024]{1,0:T(8,128)(2,1)S(1)}, bf16[512,1024]{1,0:T(8,128)(2,1)S(1)}) fusion(s32[1024]{0:T(1024)S(1)} %iota_add_fusion.4, s32[512]{0:T(512)S(1)} %iota_add_fusion.5), kind=kLoop, calls=%fused_computation.17.clone.1 | loop fusion | flops 8912896 | bytes 2103296 | tf_op jit(solution)/shard_map/convert
  279.3 1.2 copy.13
  280.5 30.8 %all-reduce.2.cloned.1.call-done = f32[16,9,1024]{2,0,1:T(8,128)} async-done(((f32[16,9,1024]{2,0,1:T(8,128)}), f32[16,9,1024]{2,0,1:T(8,128)}) %all-reduce.2.cloned.1.call-update) | async-done | bytes 589840 | tf_op jit(solution)/shard_map/psum | solution.py:77
  311.3 2.0 multiply_multiply_fusion
  (164 shorter events, 32.5 us)
Async XLA Ops:
  6.5 2.4 copy-start.1
  6.5 3.4 %copy-start.2 = (s32[16]{0:T(128)S(1)}, s32[16]{0:T(128)}, u32[]{:S(2)}) copy-start(s32[16]{0:T(128)} %param.7) | copy-start | bytes 196
  6.5 68.0 %all-gather.2.cloned.1.call-start = ((), (), s32[]{:S(2)}) async-start(), calls=%async_computation | async-start | bytes 3932160 | tf_op jit(solution)/shard_map/all_gather | solution.py:59
  7.3 304.0 %all-reduce.2.cloned.1.call-start = ((), (), s32[]{:S(2)}) async-start(), calls=%async_computation.1 | async-start | bytes 1179648 | tf_op jit(solution)/shard_map/psum | solution.py:77
  94.0 4.2 %copy-start = (f32[144,1024]{1,0:T(8,128)S(1)}, f32[144,1024]{1,0:T(8,128)}, u32[]{:S(2)}) copy-start(f32[144,1024]{1,0:T(8,128)} %custom-call) | copy-start | bytes 1769476
Sparse Core Ops, SparseCore 0:
  8.9 65.5 all-gather.1
  280.6 30.6 all-reduce.1
where the time goes:
time: 323 us; the launch traced here: 320 us
  other arithmetic  176 us (54%)
  waiting for transfers between devices  95.3 us (30%)
  local copies, waits for them, and re-layouts  24.8 us (8%)
  between operations  13.5 us (4%)
  matrix products  9.26 us (3%)
    another operation x32, other arithmetic  148 us
    all_gather x1, waiting for transfers between devices, body(): lax.all_gather(spectra, 'sta', axis=1, tiled=True)  63.7 us
    psum x1, waiting for transfers between devices, body(): stacked_sum = lax.psum(local_sum, 'hr')  30.8 us
    convert_element_type x16, other arithmetic, cross_block(): recv_part = rcv_blk.astype(jnp.float32)  16.4 us
    dot_general x16, matrix products, add_block(): return running + jnp.dot(cross, table, preferred_element_type=jnp.float32)  9.26 us
  transfers between devices with their start and end apart: 2, of which 2 were waited for; matrix products, arithmetic and copies ran while one was open for 1% of the time, Pallas kernels for 0%

commit v1 on v0

v1 whole, which is shorter than its diff:
```python
import functools
import math

import jax
import jax.numpy as jnp
import numpy as np
from jax import lax
from jax.experimental import pallas as pl
from jax.experimental.pallas import tpu as pltpu
from jax.sharding import PartitionSpec as P

LAGS = 1024
STEP = 64
two_pi = 2.0 * math.pi
MESH = pl.DeviceIdType.MESH


def angle_tables(num_bins):
    period = 2 * num_bins
    shift = np.arange(LAGS) - LAGS // 2

    def pair(bins):
        angles = np.mod(bins[:, None] * shift[None, :], period) * (two_pi / period)
        return np.cos(angles).astype(np.float32), np.sin(angles).astype(np.float32)

    return pair(np.arange(0, num_bins, STEP)) + pair(np.arange(STEP))


def window_taper():
    lag_pos = np.arange(LAGS, dtype=np.float64)
    return 0.75 - 0.25 * np.cos(two_pi * (lag_pos + 0.5) / LAGS)


def kernel(
    n, groups, hours, pairs, chunk, chunks,
    spec_ref, pick_ref, coarse_cos, coarse_sin, fine_cos, fine_sin, taper_ref,
    out_ref,
    gathered, picks, table, src, rcv, cross, acc, partial, landed, final,
    send_sem, recv_sem, pick_send, pick_recv, part_send, part_recv, fin_send, fin_recv,
):
    z = lax.axis_index("sta")
    g = lax.axis_index("grp")
    h = lax.axis_index("hr")
    plane = groups * hours
    me = g * hours + h
    block = spec_ref.shape[0]
    pick_rows = pick_ref.shape[0]
    rows = 9 * pairs
    part = LAGS // hours

    barrier = pltpu.get_barrier_semaphore()

    @pl.loop(1, plane)
    def _(d):
        t = lax.rem(me + d, plane)
        pl.semaphore_signal(
            barrier, inc=1, device_id={"grp": t // hours, "hr": lax.rem(t, hours)}, device_id_type=MESH
        )

    @pl.when(z > 0)
    def _():
        pl.semaphore_signal(barrier, inc=1, device_id={"sta": z - 1}, device_id_type=MESH)

    @pl.when(z < n - 1)
    def _():
        pl.semaphore_signal(barrier, inc=1, device_id={"sta": z + 1}, device_id_type=MESH)

    pl.semaphore_wait(barrier, plane - 1 + (z > 0).astype(jnp.int32) + (z < n - 1).astype(jnp.int32))

    def at_chunk(ref, b, c):
        return ref.at[pl.ds(pl.multiple_of(b * block, 16), block), pl.ds(pl.multiple_of(c * chunk, 128), chunk)]

    def line_copy(b, c, side, own):
        return pltpu.make_async_remote_copy(
            src_ref=at_chunk(spec_ref, 0, c) if own else at_chunk(gathered, b, c),
            dst_ref=at_chunk(gathered, b, c),
            send_sem=send_sem.at[side, b, c],
            recv_sem=recv_sem.at[b, c],
            device_id={"sta": z + 1 if side == 0 else z - 1},
            device_id_type=MESH,
        )

    @pl.loop(0, chunks)
    def _(c):
        @pl.when(z < n - 1)
        def _():
            line_copy(z, c, 0, True).start()

        @pl.when(z > 0)
        def _():
            line_copy(z, c, 1, True).start()

    def pick_copy(d):
        return pltpu.make_async_remote_copy(
            src_ref=pick_ref,
            dst_ref=picks.at[g],
            send_sem=pick_send.at[d],
            recv_sem=pick_recv.at[d],
            device_id={"grp": lax.rem(g + d, groups)},
            device_id_type=MESH,
        )

    @pl.loop(1, groups)
    def _(d):
        pick_copy(d).start()

    picks[g] = pick_ref[...]
    gathered[pl.ds(pl.multiple_of(z * block, 16), block), :] = spec_ref[...]
    acc[...] = jnp.zeros_like(acc)

    def arrive(k, c):
        @pl.when(z - k >= 0)
        def _():
            line_copy(z - k, c, 0, False).wait_recv()

            @pl.when(z < n - 1)
            def _():
                line_copy(z - k, c, 0, False).start()

        @pl.when(z + k < n)
        def _():
            line_copy(z + k, c, 1, False).wait_recv()

            @pl.when(z > 0)
            def _():
                line_copy(z + k, c, 1, False).start()

    steps = chunk // STEP

    def make_table(c):
        @pl.loop(0, steps)
        def _(i):
            row = g * (chunks * steps) + c * steps + i
            ca = coarse_cos[pl.ds(row, 1), :]
            sa = coarse_sin[pl.ds(row, 1), :]
            at = pl.multiple_of(c * (2 * chunk) + i * STEP, STEP)
            for r in range(0, STEP, 16):
                cb = fine_cos[r:r + 16, :]
                sb = fine_sin[r:r + 16, :]
                table[pl.ds(at + r, 16), :] = (ca * cb - sa * sb).astype(jnp.bfloat16)
                table[pl.ds(at + chunk + r, 16), :] = -(sa * cb + ca * sb).astype(jnp.bfloat16)

    def compute(c):
        here = pl.ds(pl.multiple_of(c * chunk, 128), chunk)
        own = spec_ref[:, here]
        every = gathered[:, here]
        for q in range(groups):
            src[q * pick_rows:(q + 1) * pick_rows, :] = jnp.dot(
                picks[q, :, n * block:(n + 1) * block], own, preferred_element_type=jnp.float32
            )
            rcv[q * pick_rows:(q + 1) * pick_rows, :] = jnp.dot(
                picks[q, :, 0:n * block], every, preferred_element_type=jnp.float32
            )

        @pl.loop(0, groups)
        def _(q):
            base = pl.multiple_of(q * pick_rows, 16)
            top = pl.multiple_of(q * rows, 16)
            for lane in range(0, chunk, 128):
                s = [src[pl.ds(base + pairs * k, pairs), lane:lane + 128] for k in range(6)]
                r = [rcv[pl.ds(base + pairs * k, pairs), lane:lane + 128] for k in range(6)]
                for a in range(3):
                    for b in range(3):
                        spot = pl.ds(top + (3 * a + b) * pairs, pairs)
                        cross[spot, lane:lane + 128] = (s[a] * r[b] + s[3 + a] * r[3 + b]).astype(jnp.bfloat16)
                        cross[spot, chunk + lane:chunk + lane + 128] = (
                            s[a] * r[3 + b] - s[3 + a] * r[b]
                        ).astype(jnp.bfloat16)

        acc[...] += jnp.dot(
            cross[...],
            table[pl.ds(pl.multiple_of(c * (2 * chunk), 16), 2 * chunk), :],
            preferred_element_type=jnp.float32,
        )

    @pl.loop(0, chunks)
    def _(c):
        make_table(c)
        arrive(1, c)

    @pl.loop(2, n - 1)
    def _(k):
        @pl.loop(0, chunks)
        def _(c):
            arrive(k, c)

    @pl.loop(1, groups)
    def _(d):
        pick_copy(d).wait()

    @pl.loop(0, chunks)
    def _(c):
        if n > 2:
            arrive(n - 1, c)
        compute(c)

    partial[...] = acc[...].astype(jnp.bfloat16)

    def part_copy(d):
        t = lax.rem(me + d, plane)
        tg, th = t // hours, lax.rem(t, hours)
        return pltpu.make_async_remote_copy(
            src_ref=partial.at[pl.ds(pl.multiple_of(tg * rows, 16), rows), pl.ds(pl.multiple_of(th * part, 128), part)],
            dst_ref=landed.at[d],
            send_sem=part_send.at[d],
            recv_sem=part_recv.at[d],
            device_id={"grp": tg, "hr": th},
            device_id_type=MESH,
        )

    @pl.loop(1, plane)
    def _(d):
        part_copy(d).start()

    lags = pl.ds(pl.multiple_of(h * part, 128), part)
    final[...] = acc[pl.ds(pl.multiple_of(g * rows, 16), rows), lags]

    @pl.loop(1, plane)
    def _(d):
        part_copy(d).wait_recv()
        final[...] += landed[d].astype(jnp.float32)

    out_ref[:, lags] = (final[...] * taper_ref[:, lags]).astype(jnp.bfloat16)

    def fin_copy(d):
        return pltpu.make_async_remote_copy(
            src_ref=out_ref.at[:, lags],
            dst_ref=out_ref.at[:, lags],
            send_sem=fin_send.at[d],
            recv_sem=fin_recv.at[d],
            device_id={"hr": lax.rem(h + d, hours)},
            device_id_type=MESH,
        )

    @pl.loop(1, hours)
    def _(d):
        fin_copy(d).start()

    @pl.loop(1, plane)
    def _(d):
        part_copy(d).wait_send()

    @pl.loop(0, n - 1)
    def _(k):
        @pl.loop(0, chunks)
        def _(c):
            @pl.when((z - k >= 0) & (z < n - 1))
            def _():
                line_copy(z - k, c, 0, True).wait_send()

            @pl.when((z + k < n) & (z > 0))
            def _():
                line_copy(z + k, c, 1, True).wait_send()

    @pl.loop(1, hours)
    def _(d):
        fin_copy(d).wait()


def body(n, groups, hours, spectra, pair_source, pair_owner, pair_row):
    _, sta_dev, comps, num_bins = spectra.shape
    pairs = pair_source.shape[0]
    bins = num_bins // groups
    chunk = min(512, bins)
    chunks = bins // chunk
    block = comps * sta_dev
    pick_rows = comps * pairs
    width = -(-((n + 1) * block) // 128) * 128

    start = lax.axis_index("grp") * bins
    mine = lax.dynamic_slice_in_dim(spectra[0], start, bins, 2)
    spec = jnp.transpose(mine, (1, 0, 2)).reshape(block, bins)

    comp_at = (jnp.arange(comps, dtype=jnp.int32) * sta_dev)[:, None]
    wanted = (comp_at + (pair_owner[:, 0] * block + pair_row)[None, :]).reshape(pick_rows, 1)
    origin = (comp_at + (n * block + pair_source)[None, :]).reshape(pick_rows, 1)
    column = jnp.arange(width, dtype=jnp.int32)[None, :]
    pick = ((wanted == column) | (origin == column)).astype(jnp.bfloat16)

    taper = (window_taper() / (hours * spectra.shape[0] * math.sqrt(num_bins))).astype(np.float32)[None, :]
    tables = angle_tables(num_bins)
    rows = 9 * pairs
    plane = groups * hours
    vmem = pl.BlockSpec(memory_space=pltpu.VMEM)
    out = pl.pallas_call(
        functools.partial(kernel, n, groups, hours, pairs, chunk, chunks),
        out_shape=jax.ShapeDtypeStruct((rows, LAGS), jnp.bfloat16),
        in_specs=[vmem] * 7,
        out_specs=vmem,
        scratch_shapes=[
            pltpu.VMEM((n * block, bins), jnp.bfloat16),
            pltpu.VMEM((groups, pick_rows, width), jnp.bfloat16),
            pltpu.VMEM((2 * bins, LAGS), jnp.bfloat16),
            pltpu.VMEM((groups * pick_rows, chunk), jnp.float32),
            pltpu.VMEM((groups * pick_rows, chunk), jnp.float32),
            pltpu.VMEM((groups * rows, 2 * chunk), jnp.bfloat16),
            pltpu.VMEM((groups * rows, LAGS), jnp.float32),
            pltpu.VMEM((groups * rows, LAGS), jnp.bfloat16),
            pltpu.VMEM((plane, rows, LAGS // hours), jnp.bfloat16),
            pltpu.VMEM((rows, LAGS // hours), jnp.float32),
            pltpu.SemaphoreType.DMA((2, n, chunks)),
            pltpu.SemaphoreType.DMA((n, chunks)),
            pltpu.SemaphoreType.DMA((groups,)),
            pltpu.SemaphoreType.DMA((groups,)),
            pltpu.SemaphoreType.DMA((plane,)),
            pltpu.SemaphoreType.DMA((plane,)),
            pltpu.SemaphoreType.DMA((hours,)),
            pltpu.SemaphoreType.DMA((hours,)),
        ],
        compiler_params=pltpu.CompilerParams(
            collective_id=0, has_side_effects=True, vmem_limit_bytes=48 * 1024 * 1024
        ),
        cost_estimate=pl.CostEstimate(
            flops=4 * groups * rows * bins * LAGS, bytes_accessed=4 * block * bins, transcendentals=0
        ),
    )(spec, pick, *[jnp.asarray(t) for t in tables], jnp.asarray(taper))
    return jnp.transpose(out.reshape(9, pairs, LAGS), (1, 0, 2)).astype(jnp.float32)


def solution(mesh):
    placed = (
        P("hr", "sta", None, None),
        P(("sta", "grp")),
        P(("sta", "grp"), None),
        P(("sta", "grp")),
    )
    sizes = (mesh.shape["sta"], mesh.shape["grp"], mesh.shape["hr"])
    return jax.shard_map(
        functools.partial(body, *sizes),
        mesh=mesh,
        in_specs=placed,
        out_specs=P(("sta", "grp"), None, None),
        check_vma=False,
    )
```

time: 323 us -> 53.2 us (0.16)
  other arithmetic: 176 us -> 1.84 us
  waiting for transfers between devices: 95.3 us -> 0 us
  Pallas kernels: 0 us -> 47.9 us
  local copies, waits for them, and re-layouts: 24.8 us -> 3.17 us
  between operations: 13.5 us -> 0.03 us
  matrix products: 9.26 us -> 0 us
    another operation x33 -> x0, other arithmetic: 148 us -> none
    all_gather x1 -> x0, waiting for transfers between devices: 63.7 us -> none  [body(): lax.all_gather(spectra, 'sta', axis=1, tiled=True)]
    pallas_call x0 -> x1, Pallas kernels: none -> 47.9 us  [body(): pl.pallas_call(functools.partial(kernel, n, groups, hours, pairs, chunk,...]
    psum x1 -> x0, waiting for transfers between devices: 30.8 us -> none  [body(): stacked_sum = lax.psum(local_sum, 'hr')]
    convert_element_type x17 -> x2, other arithmetic: 16.5 us -> 0.97 us  [the longest x1 0.87 us: body(): jnp.transpose(out.reshape(9, pairs, LAGS), (1, 0, 2)).astype(jnp.float32)]
    gather x3 -> x0, local copies, waits for them, and re-layouts: 9.84 us -> none  [the longest x1 4.99 us: body(): jnp.take(lax.all_gather(spectra, 'sta', axis=1, tiled=True), wanted_stati...]
    dot_general x16 -> x0, matrix products: 9.26 us -> none  [add_block(): return running + jnp.dot(cross, table, preferred_element_type=jnp.float32)]
    select_n x3 -> x0, other arithmetic: 8.99 us -> none  [the longest x1 4.77 us: body(): jnp.take(lax.all_gather(spectra, 'sta', axis=1, tiled=True), wanted_stati...]
  transfers between devices with their start and end apart: 2 -> 0, of which waited for: 2 -> 0; matrix products, arithmetic and copies ran while one was open for 1% -> 0% of each run, Pallas kernels for 0% -> 0%
where the time goes in v1:
time: 53.2 us; the launch traced here: 53 us
  Pallas kernels  47.9 us (90%)
  local copies, waits for them, and re-layouts  3.17 us (6%)
  other arithmetic  1.84 us (3%)
    pallas_call x1, Pallas kernels, body(): pl.pallas_call(functools.partial(kernel, n, groups, hours, pairs, chunk,...  47.9 us
    unnamed x12, local copies, waits for them, and re-layouts  2.98 us

profile of v1, /device:TPU:1, one launch (start us, length us, event | category | flops | bytes accessed | tf_op | source)
XLA Modules:
  0.0 53.0 jit_solution(3618955899107061117)
XLA Ops:
  0.0 0.0 copy-start
  0.0 0.0 copy-start.1
  0.0 0.8 %bitcast_add_fusion = (s32[16]{0:T(128)S(1)}, s32[16]{0:T(128)S(1)}) fusion(s32[16]{0:T(128)} %param.12, s32[16,1]{0,1:T(1,128)} %param.11, s32[16]{0:T(128)} %param.10), kind=kLoop, calls=%fused_computation.8 | loop fusion | flops 48 | bytes 320 | tf_op jit(solution)/shard_map/add | solution.py:275
  0.8 0.1 broadcast_add_fusion.1
  0.9 0.1 add.54
  1.0 0.1 add.58
  1.0 0.1 fusion.1.pick_ref
  1.1 0.0 copy-done
  1.2 0.0 copy-start.3
  1.2 0.0 copy-start.5
  1.2 0.1 copy-done.1
  1.3 0.8 %copy-done.3 = f32[64,1024]{1,0:T(8,128)S(1)} copy-done((f32[64,1024]{1,0:T(8,128)S(1)}, f32[64,1024]{1,0:T(8,128)}, u32[]{:S(2)}) %copy-start.3) | copy-done | bytes 262168
  2.2 0.0 copy-done.5
  2.2 0.0 copy-start.2
  2.2 1.0 %copy-done.2 = f32[128,1024]{1,0:T(8,128)S(1)} copy-done((f32[128,1024]{1,0:T(8,128)S(1)}, f32[128,1024]{1,0:T(8,128)}, u32[]{:S(2)}) %copy-start.2) | copy-done | bytes 524312
  3.2 0.0 copy-start.4
  3.2 0.9 %copy-done.4 = f32[64,1024]{1,0:T(8,128)S(1)} copy-done((f32[64,1024]{1,0:T(8,128)S(1)}, f32[64,1024]{1,0:T(8,128)}, u32[]{:S(2)}) %copy-start.4) | copy-done | bytes 262168
  4.2 47.9 %shard_map.91 = bf16[144,1024]{1,0:T(8,128)(2,1)S(1)} custom-call(bf16[48,4096]{1,0:T(8,128)(2,1)S(1)} %dynamic-slice_bitcast_fusion.spec_ref, bf16[96,256]{1,0:T(8,128)(2,1)S(1)} %fusion.1.pick_ref, f32[128,1024]{1,0:T(8,128)S(1)} %copy-done.2, f32[128,1024]{1,0:T(8,128)S(1)} %copy-done.1, f32[64,1024]{1,0:T(8,128)S(1)} %copy-done.4, ...), custom_call_target="tpu_custom_call" | custom-call | flops 4831838208 | bytes 786432 | tf_op jit(solution)/shard_map/pallas_call | solution.py:285
  52.1 0.9 %convert_bitcast_fusion = f32[16,9,1024]{2,0,1:T(8,128)} fusion(bf16[9,16,1024]{2,1,0:T(8,128)(2,1)S(1)} %bitcast.12), kind=kLoop, calls=%fused_computation | loop fusion | flops 147456 | bytes 884736 | tf_op jit(solution)/shard_map/convert_element_type | solution.py:317
  (2 shorter events, 0.0 us)
Async XLA Ops:
  0.0 1.2 %copy-start = (bf16[1,8,6,8192]{3,1,2,0:T(8,128)(2,1)S(1)}, bf16[1,8,6,8192]{3,1,2,0:T(8,128)(2,1)}, u32[]{:S(2)}) copy-start(bf16[1,8,6,8192]{3,1,2,0:T(8,128)(2,1)} %param.9) | copy-start | bytes 2359300
  0.0 1.3 %copy-start.1 = (f32[128,1024]{1,0:T(8,128)S(1)}, f32[128,1024]{1,0:T(8,128)}, u32[]{:S(2)}) copy-start(f32[128,1024]{1,0:T(8,128)} %constant.30.clone.coarse_sin) | copy-start | bytes 1572868
  1.2 1.0 %copy-start.3 = (f32[64,1024]{1,0:T(8,128)S(1)}, f32[64,1024]{1,0:T(8,128)}, u32[]{:S(2)}) copy-start(f32[64,1024]{1,0:T(8,128)} %constant.32.clone.fine_sin) | copy-start | bytes 786436
  1.2 1.0 %copy-start.5 = (f32[1,1024]{1,0:T(1,128)S(1)}, f32[1,1024]{1,0:T(1,128)}, u32[]{:S(2)}) copy-start(f32[1,1024]{1,0:T(1,128)} %constant.33.clone.taper_ref) | copy-start | bytes 12292
  2.2 1.0 %copy-start.2 = (f32[128,1024]{1,0:T(8,128)S(1)}, f32[128,1024]{1,0:T(8,128)}, u32[]{:S(2)}) copy-start(f32[128,1024]{1,0:T(8,128)} %constant.29.clone.coarse_cos) | copy-start | bytes 1572868
  3.2 0.9 %copy-start.4 = (f32[64,1024]{1,0:T(8,128)S(1)}, f32[64,1024]{1,0:T(8,128)}, u32[]{:S(2)}) copy-start(f32[64,1024]{1,0:T(8,128)} %constant.31.clone.fine_cos) | copy-start | bytes 786436

commit v2 on v1

--- a/solution.py
+++ b/solution.py
@@ -32,11 +32,13 @@
 
 
 def kernel(
-    n, groups, hours, pairs, chunk, chunks,
-    spec_ref, pick_ref, coarse_cos, coarse_sin, fine_cos, fine_sin, taper_ref,
+    n, groups, hours, pairs, chunk, chunks, helped, ahead,
+    spec_ref, pick_ref, tables_ref, taper_ref,
     out_ref,
-    gathered, picks, table, src, rcv, cross, acc, partial, landed, final,
-    send_sem, recv_sem, pick_send, pick_recv, part_send, part_recv, fin_send, fin_recv,
+    gathered, picks, coarse_cos, coarse_sin, fine_cos, fine_sin, table, src, rcv, cross, acc, partial, landed, final,
+    handed,
+    send_sem, recv_sem, pick_send, pick_recv, give_send, give_recv, part_send, part_recv, fin_send, fin_recv,
+    hand_send, hand_recv, table_sem,
 ):
     z = lax.axis_index("sta")
     g = lax.axis_index("grp")
@@ -47,6 +49,26 @@
     pick_rows = pick_ref.shape[0]
     rows = 9 * pairs
     part = LAGS // hours
+    steps = chunk // STEP
+    edge = (z == 0) | (z == n - 1)
+    helper = (z == 1) | (z == n - 2)
+    partner = jnp.where(z == 0, 1, jnp.where(z == 1, 0, jnp.where(z == n - 1, n - 2, n - 1)))
+
+    def table_copy(i):
+        if i < 2:
+            rows_here = chunks * steps
+            first = i * (groups * rows_here) + g * rows_here
+            return pltpu.make_async_copy(
+                tables_ref.at[pl.ds(pl.multiple_of(first, 8), rows_here)],
+                (coarse_cos, coarse_sin)[i], table_sem.at[i],
+            )
+        first = 2 * groups * chunks * steps + (i - 2) * STEP
+        return pltpu.make_async_copy(
+            tables_ref.at[pl.ds(first, STEP)], (fine_cos, fine_sin)[i - 2], table_sem.at[i]
+        )
+
+    for i in range(4):
+        table_copy(i).start()
 
     barrier = pltpu.get_barrier_semaphore()
 
@@ -65,7 +87,18 @@
     def _():
         pl.semaphore_signal(barrier, inc=1, device_id={"sta": z + 1}, device_id_type=MESH)
 
-    pl.semaphore_wait(barrier, plane - 1 + (z > 0).astype(jnp.int32) + (z < n - 1).astype(jnp.int32))
+    expected = plane - 1 + (z > 0).astype(jnp.int32) + (z < n - 1).astype(jnp.int32)
+    if helped:
+        @pl.when(edge | helper)
+        def _():
+            @pl.loop(1, groups)
+            def _(d):
+                pl.semaphore_signal(
+                    barrier, inc=1, device_id={"sta": partner, "grp": lax.rem(g + d, groups)}, device_id_type=MESH
+                )
+
+        expected = expected + (groups - 1) * (edge | helper).astype(jnp.int32)
+    pl.semaphore_wait(barrier, expected)
 
     def at_chunk(ref, b, c):
         return ref.at[pl.ds(pl.multiple_of(b * block, 16), block), pl.ds(pl.multiple_of(c * chunk, 128), chunk)]
@@ -80,57 +113,83 @@
             device_id_type=MESH,
         )
 
-    @pl.loop(0, chunks)
-    def _(c):
-        @pl.when(z < n - 1)
+    def goes_right(c):
+        return (z < n - 2) | ((z == n - 2) & (c >= helped))
+
+    def goes_left(c):
+        return (z > 1) | ((z == 1) & (c >= helped))
+
+    def send_own(c):
+        @pl.when(goes_right(c))
         def _():
             line_copy(z, c, 0, True).start()
 
-        @pl.when(z > 0)
+        @pl.when(goes_left(c))
         def _():
             line_copy(z, c, 1, True).start()
 
     def pick_copy(d):
         return pltpu.make_async_remote_copy(
             src_ref=pick_ref,
-            dst_ref=picks.at[g],
+            dst_ref=picks.at[0, pl.ds(pl.multiple_of(g * pick_rows, 16), pick_rows)],
             send_sem=pick_send.at[d],
             recv_sem=pick_recv.at[d],
             device_id={"grp": lax.rem(g + d, groups)},
             device_id_type=MESH,
         )
 
+    def give_copy(d):
+        return pltpu.make_async_remote_copy(
+            src_ref=pick_ref,
+            dst_ref=picks.at[1, pl.ds(pl.multiple_of(g * pick_rows, 16), pick_rows)],
+            send_sem=give_send.at[d],
+            recv_sem=give_recv.at[d],
+            device_id={"sta": partner, "grp": lax.rem(g + d, groups)},
+            device_id_type=MESH,
+        )
+
+    @pl.loop(0, min(ahead, chunks))
+    def _(c):
+        send_own(c)
+
     @pl.loop(1, groups)
     def _(d):
         pick_copy(d).start()
 
-    picks[g] = pick_ref[...]
+    if helped:
+        @pl.when(edge)
+        def _():
+            @pl.loop(0, groups)
+            def _(d):
+                give_copy(d).start()
+
+    picks[0, pl.ds(pl.multiple_of(g * pick_rows, 16), pick_rows), :] = pick_ref[...]
     gathered[pl.ds(pl.multiple_of(z * block, 16), block), :] = spec_ref[...]
     acc[...] = jnp.zeros_like(acc)
 
     def arrive(k, c):
-        @pl.when(z - k >= 0)
+        wanted = (c >= helped) | jnp.logical_not(edge)
+
+        @pl.when((z - k >= 0) & wanted)
         def _():
             line_copy(z - k, c, 0, False).wait_recv()
 
-            @pl.when(z < n - 1)
+            @pl.when(goes_right(c))
             def _():
                 line_copy(z - k, c, 0, False).start()
 
-        @pl.when(z + k < n)
+        @pl.when((z + k < n) & wanted)
         def _():
             line_copy(z + k, c, 1, False).wait_recv()
 
-            @pl.when(z > 0)
+            @pl.when(goes_left(c))
             def _():
                 line_copy(z + k, c, 1, False).start()
-
-    steps = chunk // STEP
 
     def make_table(c):
         @pl.loop(0, steps)
         def _(i):
-            row = g * (chunks * steps) + c * steps + i
+            row = c * steps + i
             ca = coarse_cos[pl.ds(row, 1), :]
             sa = coarse_sin[pl.ds(row, 1), :]
             at = pl.multiple_of(c * (2 * chunk) + i * STEP, STEP)
@@ -140,17 +199,16 @@
                 table[pl.ds(at + r, 16), :] = (ca * cb - sa * sb).astype(jnp.bfloat16)
                 table[pl.ds(at + chunk + r, 16), :] = -(sa * cb + ca * sb).astype(jnp.bfloat16)
 
-    def compute(c):
+    def compute(w, c):
         here = pl.ds(pl.multiple_of(c * chunk, 128), chunk)
-        own = spec_ref[:, here]
-        every = gathered[:, here]
-        for q in range(groups):
-            src[q * pick_rows:(q + 1) * pick_rows, :] = jnp.dot(
-                picks[q, :, n * block:(n + 1) * block], own, preferred_element_type=jnp.float32
-            )
-            rcv[q * pick_rows:(q + 1) * pick_rows, :] = jnp.dot(
-                picks[q, :, 0:n * block], every, preferred_element_type=jnp.float32
-            )
+        origin = jnp.where(w == 0, z, partner)
+        own = gathered[pl.ds(pl.multiple_of(origin * block, 16), block), here]
+        src[...] = jnp.dot(
+            picks[w, :, n * block:(n + 1) * block], own, preferred_element_type=jnp.float32
+        )
+        rcv[...] = jnp.dot(
+            picks[w, :, 0:n * block], gathered[:, here], preferred_element_type=jnp.float32
+        )
 
         @pl.loop(0, groups)
         def _(q):
@@ -167,58 +225,115 @@
                             s[a] * r[3 + b] - s[3 + a] * r[b]
                         ).astype(jnp.bfloat16)
 
-        acc[...] += jnp.dot(
+        acc[w] += jnp.dot(
             cross[...],
             table[pl.ds(pl.multiple_of(c * (2 * chunk), 16), 2 * chunk), :],
             preferred_element_type=jnp.float32,
         )
 
-    @pl.loop(0, chunks)
-    def _(c):
-        make_table(c)
-        arrive(1, c)
-
-    @pl.loop(2, n - 1)
-    def _(k):
-        @pl.loop(0, chunks)
-        def _(c):
-            arrive(k, c)
-
-    @pl.loop(1, groups)
-    def _(d):
-        pick_copy(d).wait()
-
-    @pl.loop(0, chunks)
-    def _(c):
-        if n > 2:
-            arrive(n - 1, c)
-        compute(c)
-
-    partial[...] = acc[...].astype(jnp.bfloat16)
-
-    def part_copy(d):
+    lags = pl.ds(pl.multiple_of(h * part, 128), part)
+    own_rows = pl.ds(pl.multiple_of(g * rows, 16), rows)
+
+    def part_copy(w, d):
         t = lax.rem(me + d, plane)
         tg, th = t // hours, lax.rem(t, hours)
         return pltpu.make_async_remote_copy(
-            src_ref=partial.at[pl.ds(pl.multiple_of(tg * rows, 16), rows), pl.ds(pl.multiple_of(th * part, 128), part)],
-            dst_ref=landed.at[d],
-            send_sem=part_send.at[d],
-            recv_sem=part_recv.at[d],
+            src_ref=partial.at[
+                w, pl.ds(pl.multiple_of(tg * rows, 16), rows), pl.ds(pl.multiple_of(th * part, 128), part)
+            ],
+            dst_ref=landed.at[w, d],
+            send_sem=part_send.at[w, d],
+            recv_sem=part_recv.at[w, d],
             device_id={"grp": tg, "hr": th},
             device_id_type=MESH,
         )
 
-    @pl.loop(1, plane)
-    def _(d):
-        part_copy(d).start()
-
-    lags = pl.ds(pl.multiple_of(h * part, 128), part)
-    final[...] = acc[pl.ds(pl.multiple_of(g * rows, 16), rows), lags]
-
-    @pl.loop(1, plane)
-    def _(d):
-        part_copy(d).wait_recv()
-        final[...] += landed[d].astype(jnp.float32)
+    def scatter(w):
+        partial[w] = acc[w].astype(jnp.bfloat16)
+
+        @pl.loop(1, plane)
+        def _(d):
+            part_copy(w, d).start()
+
+    def collect(w):
+        final[...] = acc[w, own_rows, lags]
+
+        @pl.loop(1, plane)
+        def _(d):
+            part_copy(w, d).wait_recv()
+            final[...] += landed[w, d].astype(jnp.float32)
+
+    def hand_copy():
+        return pltpu.make_async_remote_copy(
+            src_ref=handed,
+            dst_ref=landed.at[0, 0],
+            send_sem=hand_send,
+            recv_sem=hand_recv,
+            device_id={"sta": partner},
+            device_id_type=MESH,
+        )
+
+    for i in range(4):
+        table_copy(i).wait()
+
+    lag_steps = max(n - 2, 0)
+
+    @pl.loop(0, chunks + lag_steps)
+    def _(it):
+        @pl.when(it + ahead < chunks)
+        def _():
+            send_own(it + ahead)
+
+        @pl.when((it < chunks) & ((it >= helped) | jnp.logical_not(edge)))
+        def _():
+            make_table(it)
+
+        @pl.loop(1, n)
+        def _(k):
+            c = it - (k - 1)
+
+            @pl.when((c >= 0) & (c < chunks))
+            def _():
+                arrive(k, c)
+
+        @pl.when(it == lag_steps)
+        def _():
+            @pl.loop(1, groups)
+            def _(d):
+                pick_copy(d).wait()
+
+            if helped:
+                @pl.when(helper)
+                def _():
+                    @pl.loop(0, groups)
+                    def _(d):
+                        give_copy(d).wait_recv()
+
+        c = it - lag_steps
+        turns = jnp.where(c >= helped, 1, jnp.where(edge, 0, jnp.where(helper, 2, 1)))
+
+        @pl.loop(0, jnp.where(c >= 0, turns, 0))
+        def _(w):
+            compute(w, c)
+
+        if helped:
+            @pl.when(helper & (c == helped - 1))
+            def _():
+                scatter(1)
+
+            @pl.when(helper & (c == helped + 1))
+            def _():
+                collect(1)
+                handed[...] = final[...].astype(jnp.bfloat16)
+                hand_copy().start()
+
+    scatter(0)
+    collect(0)
+    if helped:
+        @pl.when(edge)
+        def _():
+            hand_copy().wait_recv()
+            final[...] += landed[0, 0].astype(jnp.float32)
 
     out_ref[:, lags] = (final[...] * taper_ref[:, lags]).astype(jnp.bfloat16)
 
@@ -238,17 +353,32 @@
 
     @pl.loop(1, plane)
     def _(d):
-        part_copy(d).wait_send()
+        part_copy(0, d).wait_send()
+
+    if helped:
+        @pl.when(helper)
+        def _():
+            hand_copy().wait_send()
+
+            @pl.loop(1, plane)
+            def _(d):
+                part_copy(1, d).wait_send()
+
+        @pl.when(edge)
+        def _():
+            @pl.loop(0, groups)
+            def _(d):
+                give_copy(d).wait_send()
 
     @pl.loop(0, n - 1)
     def _(k):
         @pl.loop(0, chunks)
         def _(c):
-            @pl.when((z - k >= 0) & (z < n - 1))
+            @pl.when((z - k >= 0) & goes_right(c))
             def _():
                 line_copy(z - k, c, 0, True).wait_send()
 
-            @pl.when((z + k < n) & (z > 0))
+            @pl.when((z + k < n) & goes_left(c))
             def _():
                 line_copy(z + k, c, 1, True).wait_send()
 
@@ -263,6 +393,8 @@
     bins = num_bins // groups
     chunk = min(512, bins)
     chunks = bins // chunk
+    helped = 3 * chunks // 8 if n >= 4 else 0
+    held = 2 if helped else 1
     block = comps * sta_dev
     pick_rows = comps * pairs
     width = -(-((n + 1) * block) // 128) * 128
@@ -282,30 +414,40 @@
     rows = 9 * pairs
     plane = groups * hours
     vmem = pl.BlockSpec(memory_space=pltpu.VMEM)
+    hbm = pl.BlockSpec(memory_space=pltpu.HBM)
+    coarse = pltpu.VMEM((bins // STEP, LAGS), jnp.float32)
+    fine = pltpu.VMEM((STEP, LAGS), jnp.float32)
     out = pl.pallas_call(
-        functools.partial(kernel, n, groups, hours, pairs, chunk, chunks),
+        functools.partial(kernel, n, groups, hours, pairs, chunk, chunks, helped, 3),
         out_shape=jax.ShapeDtypeStruct((rows, LAGS), jnp.bfloat16),
-        in_specs=[vmem] * 7,
+        in_specs=[vmem, vmem, hbm, vmem],
         out_specs=vmem,
         scratch_shapes=[
             pltpu.VMEM((n * block, bins), jnp.bfloat16),
-            pltpu.VMEM((groups, pick_rows, width), jnp.bfloat16),
+            pltpu.VMEM((held, groups * pick_rows, width), jnp.bfloat16),
+            coarse, coarse, fine, fine,
             pltpu.VMEM((2 * bins, LAGS), jnp.bfloat16),
             pltpu.VMEM((groups * pick_rows, chunk), jnp.float32),
             pltpu.VMEM((groups * pick_rows, chunk), jnp.float32),
             pltpu.VMEM((groups * rows, 2 * chunk), jnp.bfloat16),
-            pltpu.VMEM((groups * rows, LAGS), jnp.float32),
-            pltpu.VMEM((groups * rows, LAGS), jnp.bfloat16),
-            pltpu.VMEM((plane, rows, LAGS // hours), jnp.bfloat16),
+            pltpu.VMEM((held, groups * rows, LAGS), jnp.float32),
+            pltpu.VMEM((held, groups * rows, LAGS), jnp.bfloat16),
+            pltpu.VMEM((held, plane, rows, LAGS // hours), jnp.bfloat16),
             pltpu.VMEM((rows, LAGS // hours), jnp.float32),
+            pltpu.VMEM((rows, LAGS // hours), jnp.bfloat16),
             pltpu.SemaphoreType.DMA((2, n, chunks)),
             pltpu.SemaphoreType.DMA((n, chunks)),
             pltpu.SemaphoreType.DMA((groups,)),
             pltpu.SemaphoreType.DMA((groups,)),
-            pltpu.SemaphoreType.DMA((plane,)),
-            pltpu.SemaphoreType.DMA((plane,)),
+            pltpu.SemaphoreType.DMA((groups,)),
+            pltpu.SemaphoreType.DMA((groups,)),
+            pltpu.SemaphoreType.DMA((held, plane)),
+            pltpu.SemaphoreType.DMA((held, plane)),
             pltpu.SemaphoreType.DMA((hours,)),
             pltpu.SemaphoreType.DMA((hours,)),
+            pltpu.SemaphoreType.DMA,
+            pltpu.SemaphoreType.DMA,
+            pltpu.SemaphoreType.DMA((4,)),
         ],
         compiler_params=pltpu.CompilerParams(
             collective_id=0, has_side_effects=True, vmem_limit_bytes=48 * 1024 * 1024
@@ -313,7 +455,7 @@
         cost_estimate=pl.CostEstimate(
             flops=4 * groups * rows * bins * LAGS, bytes_accessed=4 * block * bins, transcendentals=0
         ),
-    )(spec, pick, *[jnp.asarray(t) for t in tables], jnp.asarray(taper))
+    )(spec, pick, jnp.asarray(np.concatenate(tables)), jnp.asarray(taper))
     return jnp.transpose(out.reshape(9, pairs, LAGS), (1, 0, 2)).astype(jnp.float32)
 
 

time: 53.2 us -> 58 us (1.090)
  Pallas kernels: 47.9 us -> 53.6 us
  local copies, waits for them, and re-layouts: 3.17 us -> 2.35 us
    pallas_call x1, Pallas kernels: 47.9 us -> 53.6 us  [body(): pl.pallas_call(functools.partial(kernel, n, groups, hours, pairs, chunk,...]
    unnamed x12 -> x6, local copies, waits for them, and re-layouts: 2.98 us -> 2.17 us
where the time goes in v2:
time: 58 us; the launch traced here: 57.8 us
  Pallas kernels  53.6 us (92%)
  local copies, waits for them, and re-layouts  2.35 us (4%)
  other arithmetic  1.81 us (3%)
    pallas_call x1, Pallas kernels, body(): pl.pallas_call(functools.partial(kernel, n, groups, hours, pairs, chunk,...  53.6 us
    unnamed x6, local copies, waits for them, and re-layouts  2.17 us

profile of v2, /device:TPU:1, one launch (start us, length us, event | category | flops | bytes accessed | tf_op | source)
XLA Modules:
  0.0 57.8 jit_solution(9717586303830822863)
XLA Ops:
  0.0 0.0 copy-start
  0.0 0.8 %bitcast_add_fusion = (s32[16]{0:T(128)S(1)}, s32[16]{0:T(128)S(1)}) fusion(s32[16]{0:T(128)} %param.9, s32[16,1]{0,1:T(1,128)} %param.8, s32[16]{0:T(128)} %param.7), kind=kLoop, calls=%fused_computation.8 | loop fusion | flops 48 | bytes 320 | tf_op jit(solution)/shard_map/add | solution.py:407
  0.8 0.1 broadcast_add_fusion.1
  0.8 0.1 add.54
  0.9 0.1 add.58
  1.0 0.1 fusion.1.pick_ref
  1.1 0.1 copy-done
  1.2 0.0 copy-start.1
  1.2 1.4 %copy-done.1 = f32[384,1024]{1,0:T(8,128)S(1)} copy-done((f32[384,1024]{1,0:T(8,128)S(1)}, f32[384,1024]{1,0:T(8,128)}, u32[]{:S(2)}) %copy-start.1) | copy-done | bytes 1572888
  2.6 0.0 copy-start.2
  2.6 0.7 %copy-done.2 = f32[1,1024]{1,0:T(1,128)S(1)} copy-done((f32[1,1024]{1,0:T(1,128)S(1)}, f32[1,1024]{1,0:T(1,128)}, u32[]{:S(2)}) %copy-start.2) | copy-done | bytes 4120
  3.3 53.6 %shard_map.64 = bf16[144,1024]{1,0:T(8,128)(2,1)S(1)} custom-call(bf16[48,4096]{1,0:T(8,128)(2,1)S(1)} %dynamic-slice_bitcast_fusion.spec_ref, bf16[96,256]{1,0:T(8,128)(2,1)S(1)} %fusion.1.pick_ref, f32[384,1024]{1,0:T(8,128)S(1)} %copy-done.1, f32[1,1024]{1,0:T(1,128)S(1)} %copy-done.2), custom_call_target="tpu_custom_call" | custom-call | flops 4831838208 | bytes 786432 | tf_op jit(solution)/shard_map/pallas_call | solution.py:420
  56.9 0.9 %convert_bitcast_fusion = f32[16,9,1024]{2,0,1:T(8,128)} fusion(bf16[9,16,1024]{2,1,0:T(8,128)(2,1)S(1)} %bitcast.12), kind=kLoop, calls=%fused_computation | loop fusion | flops 147456 | bytes 884736 | tf_op jit(solution)/shard_map/convert_element_type | solution.py:459
  (2 shorter events, 0.0 us)
Async XLA Ops:
  0.0 1.2 %copy-start = (bf16[1,8,6,8192]{3,1,2,0:T(8,128)(2,1)S(1)}, bf16[1,8,6,8192]{3,1,2,0:T(8,128)(2,1)}, u32[]{:S(2)}) copy-start(bf16[1,8,6,8192]{3,1,2,0:T(8,128)(2,1)} %param.6) | copy-start | bytes 2359300
  1.2 1.4 %copy-start.1 = (f32[384,1024]{1,0:T(8,128)S(1)}, f32[384,1024]{1,0:T(8,128)}, u32[]{:S(2)}) copy-start(f32[384,1024]{1,0:T(8,128)} %constant.23.clone.tables_ref) | copy-start | bytes 4718596
  2.6 0.7 %copy-start.2 = (f32[1,1024]{1,0:T(1,128)S(1)}, f32[1,1024]{1,0:T(1,128)}, u32[]{:S(2)}) copy-start(f32[1,1024]{1,0:T(1,128)} %constant.24.clone.taper_ref) | copy-start | bytes 12292

commit v3 on v2

--- a/solution.py
+++ b/solution.py
@@ -3,7 +3,6 @@
 
 import jax
 import jax.numpy as jnp
-import numpy as np
 from jax import lax
 from jax.experimental import pallas as pl
 from jax.experimental.pallas import tpu as pltpu
@@ -15,30 +14,22 @@
 MESH = pl.DeviceIdType.MESH
 
 
-def angle_tables(num_bins):
+def turn(first, step, num_bins):
     period = 2 * num_bins
-    shift = np.arange(LAGS) - LAGS // 2
-
-    def pair(bins):
-        angles = np.mod(bins[:, None] * shift[None, :], period) * (two_pi / period)
-        return np.cos(angles).astype(np.float32), np.sin(angles).astype(np.float32)
-
-    return pair(np.arange(0, num_bins, STEP)) + pair(np.arange(STEP))
-
-
-def window_taper():
-    lag_pos = np.arange(LAGS, dtype=np.float64)
-    return 0.75 - 0.25 * np.cos(two_pi * (lag_pos + 0.5) / LAGS)
+    bins = first + step * lax.broadcasted_iota(jnp.int32, (8, LAGS), 0)
+    shift = lax.broadcasted_iota(jnp.int32, (8, LAGS), 1) - LAGS // 2
+    angle = (((bins * shift + num_bins) & (period - 1)) - num_bins).astype(jnp.float32) * (two_pi / period)
+    return jnp.cos(angle), jnp.sin(angle)
 
 
 def kernel(
-    n, groups, hours, pairs, chunk, chunks, helped, ahead,
-    spec_ref, pick_ref, tables_ref, taper_ref,
+    n, groups, hours, pairs, chunk, chunks, helped, ahead, slack, scale,
+    spec_ref, pick_ref,
     out_ref,
     gathered, picks, coarse_cos, coarse_sin, fine_cos, fine_sin, table, src, rcv, cross, acc, partial, landed, final,
     handed,
     send_sem, recv_sem, pick_send, pick_recv, give_send, give_recv, part_send, part_recv, fin_send, fin_recv,
-    hand_send, hand_recv, table_sem,
+    hand_send, hand_recv,
 ):
     z = lax.axis_index("sta")
     g = lax.axis_index("grp")
@@ -54,21 +45,8 @@
     helper = (z == 1) | (z == n - 2)
     partner = jnp.where(z == 0, 1, jnp.where(z == 1, 0, jnp.where(z == n - 1, n - 2, n - 1)))
 
-    def table_copy(i):
-        if i < 2:
-            rows_here = chunks * steps
-            first = i * (groups * rows_here) + g * rows_here
-            return pltpu.make_async_copy(
-                tables_ref.at[pl.ds(pl.multiple_of(first, 8), rows_here)],
-                (coarse_cos, coarse_sin)[i], table_sem.at[i],
-            )
-        first = 2 * groups * chunks * steps + (i - 2) * STEP
-        return pltpu.make_async_copy(
-            tables_ref.at[pl.ds(first, STEP)], (fine_cos, fine_sin)[i - 2], table_sem.at[i]
-        )
-
-    for i in range(4):
-        table_copy(i).start()
+    for c in range(chunks):
+        gathered[c, pl.ds(pl.multiple_of(z * block, 16), block), :] = spec_ref[:, c * chunk:(c + 1) * chunk]
 
     barrier = pltpu.get_barrier_semaphore()
 
@@ -100,13 +78,11 @@
         expected = expected + (groups - 1) * (edge | helper).astype(jnp.int32)
     pl.semaphore_wait(barrier, expected)
 
-    def at_chunk(ref, b, c):
-        return ref.at[pl.ds(pl.multiple_of(b * block, 16), block), pl.ds(pl.multiple_of(c * chunk, 128), chunk)]
-
-    def line_copy(b, c, side, own):
-        return pltpu.make_async_remote_copy(
-            src_ref=at_chunk(spec_ref, 0, c) if own else at_chunk(gathered, b, c),
-            dst_ref=at_chunk(gathered, b, c),
+    def line_copy(b, c, side):
+        spot = gathered.at[c, pl.ds(pl.multiple_of(b * block, 16), block)]
+        return pltpu.make_async_remote_copy(
+            src_ref=spot,
+            dst_ref=spot,
             send_sem=send_sem.at[side, b, c],
             recv_sem=recv_sem.at[b, c],
             device_id={"sta": z + 1 if side == 0 else z - 1},
@@ -122,11 +98,11 @@
     def send_own(c):
         @pl.when(goes_right(c))
         def _():
-            line_copy(z, c, 0, True).start()
+            line_copy(z, c, 0).start()
 
         @pl.when(goes_left(c))
         def _():
-            line_copy(z, c, 1, True).start()
+            line_copy(z, c, 1).start()
 
     def pick_copy(d):
         return pltpu.make_async_remote_copy(
@@ -164,27 +140,39 @@
                 give_copy(d).start()
 
     picks[0, pl.ds(pl.multiple_of(g * pick_rows, 16), pick_rows), :] = pick_ref[...]
-    gathered[pl.ds(pl.multiple_of(z * block, 16), block), :] = spec_ref[...]
     acc[...] = jnp.zeros_like(acc)
+
+    num_bins = groups * chunks * chunk
+
+    def outer(cos_ref, sin_ref, count, first, step):
+        lc, ls = turn(0, step, num_bins)
+        hc, hs = turn(first, 8 * step, num_bins)
+        for i in range(count // 8):
+            a, b = hc[i:i + 1, :], hs[i:i + 1, :]
+            cos_ref[8 * i:8 * i + 8, :] = a * lc - b * ls
+            sin_ref[8 * i:8 * i + 8, :] = b * lc + a * ls
+
+    outer(fine_cos, fine_sin, STEP, 0, 1)
+    outer(coarse_cos, coarse_sin, chunks * steps, g * (chunks * chunk), STEP)
 
     def arrive(k, c):
         wanted = (c >= helped) | jnp.logical_not(edge)
 
         @pl.when((z - k >= 0) & wanted)
         def _():
-            line_copy(z - k, c, 0, False).wait_recv()
+            line_copy(z - k, c, 0).wait_recv()
 
             @pl.when(goes_right(c))
             def _():
-                line_copy(z - k, c, 0, False).start()
+                line_copy(z - k, c, 0).start()
 
         @pl.when((z + k < n) & wanted)
         def _():
-            line_copy(z + k, c, 1, False).wait_recv()
+            line_copy(z + k, c, 1).wait_recv()
 
             @pl.when(goes_left(c))
             def _():
-                line_copy(z + k, c, 1, False).start()
+                line_copy(z + k, c, 1).start()
 
     def make_table(c):
         @pl.loop(0, steps)
@@ -200,14 +188,13 @@
                 table[pl.ds(at + chunk + r, 16), :] = -(sa * cb + ca * sb).astype(jnp.bfloat16)
 
     def compute(w, c):
-        here = pl.ds(pl.multiple_of(c * chunk, 128), chunk)
         origin = jnp.where(w == 0, z, partner)
-        own = gathered[pl.ds(pl.multiple_of(origin * block, 16), block), here]
+        own = gathered[c, pl.ds(pl.multiple_of(origin * block, 16), block), :]
         src[...] = jnp.dot(
             picks[w, :, n * block:(n + 1) * block], own, preferred_element_type=jnp.float32
         )
         rcv[...] = jnp.dot(
-            picks[w, :, 0:n * block], gathered[:, here], preferred_element_type=jnp.float32
+            picks[w, :, 0:n * block], gathered[c], preferred_element_type=jnp.float32
         )
 
         @pl.loop(0, groups)
@@ -273,12 +260,9 @@
             device_id_type=MESH,
         )
 
-    for i in range(4):
-        table_copy(i).wait()
-
-    lag_steps = max(n - 2, 0)
-
-    @pl.loop(0, chunks + lag_steps)
+    lag_steps = slack * (jnp.maximum(z, n - 1 - z) - 1)
+
+    @pl.loop(0, chunks + slack * max(n - 2, 0))
     def _(it):
         @pl.when(it + ahead < chunks)
         def _():
@@ -290,7 +274,7 @@
 
         @pl.loop(1, n)
         def _(k):
-            c = it - (k - 1)
+            c = it - slack * (k - 1)
 
             @pl.when((c >= 0) & (c < chunks))
             def _():
@@ -312,7 +296,7 @@
         c = it - lag_steps
         turns = jnp.where(c >= helped, 1, jnp.where(edge, 0, jnp.where(helper, 2, 1)))
 
-        @pl.loop(0, jnp.where(c >= 0, turns, 0))
+        @pl.loop(0, jnp.where((c >= 0) & (c < chunks), turns, 0))
         def _(w):
             compute(w, c)
 
@@ -335,7 +319,9 @@
             hand_copy().wait_recv()
             final[...] += landed[0, 0].astype(jnp.float32)
 
-    out_ref[:, lags] = (final[...] * taper_ref[:, lags]).astype(jnp.bfloat16)
+    lag = (h * part + lax.broadcasted_iota(jnp.int32, (8, part), 1)).astype(jnp.float32)
+    taper = (0.75 - 0.25 * jnp.cos(two_pi * (lag + 0.5) / LAGS)) * scale
+    out_ref[:, lags] = (final[...] * taper[0:1, :]).astype(jnp.bfloat16)
 
     def fin_copy(d):
         return pltpu.make_async_remote_copy(
@@ -376,11 +362,11 @@
         def _(c):
             @pl.when((z - k >= 0) & goes_right(c))
             def _():
-                line_copy(z - k, c, 0, True).wait_send()
+                line_copy(z - k, c, 0).wait_send()
 
             @pl.when((z + k < n) & goes_left(c))
             def _():
-                line_copy(z + k, c, 1, True).wait_send()
+                line_copy(z + k, c, 1).wait_send()
 
     @pl.loop(1, hours)
     def _(d):
@@ -409,21 +395,19 @@
     column = jnp.arange(width, dtype=jnp.int32)[None, :]
     pick = ((wanted == column) | (origin == column)).astype(jnp.bfloat16)
 
-    taper = (window_taper() / (hours * spectra.shape[0] * math.sqrt(num_bins))).astype(np.float32)[None, :]
-    tables = angle_tables(num_bins)
+    scale = 1.0 / (hours * spectra.shape[0] * math.sqrt(num_bins))
     rows = 9 * pairs
     plane = groups * hours
     vmem = pl.BlockSpec(memory_space=pltpu.VMEM)
-    hbm = pl.BlockSpec(memory_space=pltpu.HBM)
     coarse = pltpu.VMEM((bins // STEP, LAGS), jnp.float32)
     fine = pltpu.VMEM((STEP, LAGS), jnp.float32)
     out = pl.pallas_call(
-        functools.partial(kernel, n, groups, hours, pairs, chunk, chunks, helped, 3),
+        functools.partial(kernel, n, groups, hours, pairs, chunk, chunks, helped, 3, 2, scale),
         out_shape=jax.ShapeDtypeStruct((rows, LAGS), jnp.bfloat16),
-        in_specs=[vmem, vmem, hbm, vmem],
+        in_specs=[vmem, vmem],
         out_specs=vmem,
         scratch_shapes=[
-            pltpu.VMEM((n * block, bins), jnp.bfloat16),
+            pltpu.VMEM((chunks, n * block, chunk), jnp.bfloat16),
             pltpu.VMEM((held, groups * pick_rows, width), jnp.bfloat16),
             coarse, coarse, fine, fine,
             pltpu.VMEM((2 * bins, LAGS), jnp.bfloat16),
@@ -447,7 +431,6 @@
             pltpu.SemaphoreType.DMA((hours,)),
             pltpu.SemaphoreType.DMA,
             pltpu.SemaphoreType.DMA,
-            pltpu.SemaphoreType.DMA((4,)),
         ],
         compiler_params=pltpu.CompilerParams(
             collective_id=0, has_side_effects=True, vmem_limit_bytes=48 * 1024 * 1024
@@ -455,7 +438,7 @@
         cost_estimate=pl.CostEstimate(
             flops=4 * groups * rows * bins * LAGS, bytes_accessed=4 * block * bins, transcendentals=0
         ),
-    )(spec, pick, jnp.asarray(np.concatenate(tables)), jnp.asarray(taper))
+    )(spec, pick)
     return jnp.transpose(out.reshape(9, pairs, LAGS), (1, 0, 2)).astype(jnp.float32)
 
 

time: 58 us -> 55.1 us (0.950)
  local copies, waits for them, and re-layouts: 2.35 us -> 1 us
  Pallas kernels: 53.6 us -> 52.8 us
  other arithmetic: 1.81 us -> 1.06 us
    unnamed x6 -> x8, local copies, waits for them, and re-layouts: 2.17 us -> 0.81 us
    pallas_call x1, Pallas kernels: 53.6 us -> 52.8 us  [body(): pl.pallas_call(functools.partial(kernel, n, groups, hours, pairs, chunk,...]
    add x1, other arithmetic: 0.76 us -> 0.01 us  [body(): pair_owner[:, 0] * block + pair_row]
where the time goes in v3:
time: 55.1 us; the launch traced here: 54.9 us
  Pallas kernels  52.8 us (96%)
  other arithmetic  1.06 us (2%)
  local copies, waits for them, and re-layouts  1 us (2%)
    pallas_call x1, Pallas kernels, body(): pl.pallas_call(functools.partial(kernel, n, groups, hours, pairs, chunk,...  52.8 us

profile of v3, /device:TPU:1, one launch (start us, length us, event | category | flops | bytes accessed | tf_op | source)
XLA Modules:
  0.0 54.9 jit_solution(16898720240208232674)
XLA Ops:
  0.0 0.0 copy-start
  0.0 0.0 copy-start.1
  0.0 0.0 copy-start.2
  0.0 0.0 copy-start.3
  0.0 0.7 %copy-done.1 = s32[16]{0:T(128)S(1)} copy-done((s32[16]{0:T(128)S(1)}, s32[16]{0:T(128)}, u32[]{:S(2)}) %copy-start.1) | copy-done | bytes 88
  0.7 0.0 copy-done.2
  0.7 0.0 copy-done.3
  0.8 0.1 broadcast_add_fusion.1
  0.8 0.1 add.54
  0.9 0.1 add.58
  1.0 0.1 fusion.1.pick_ref
  1.1 0.1 copy-done
  1.2 52.8 %shard_map.46 = bf16[144,1024]{1,0:T(8,128)(2,1)S(1)} custom-call(bf16[48,4096]{1,0:T(8,128)(2,1)S(1)} %dynamic-slice_bitcast_fusion.spec_ref, bf16[96,256]{1,0:T(8,128)(2,1)S(1)} %fusion.1.pick_ref), custom_call_target="tpu_custom_call" | custom-call | flops 4831838208 | bytes 786432 | tf_op jit(solution)/shard_map/pallas_call | solution.py:404
  54.0 0.9 %convert_bitcast_fusion = f32[16,9,1024]{2,0,1:T(8,128)} fusion(bf16[9,16,1024]{2,1,0:T(8,128)(2,1)S(1)} %bitcast.12), kind=kLoop, calls=%fused_computation | loop fusion | flops 147456 | bytes 884736 | tf_op jit(solution)/shard_map/convert_element_type | solution.py:442
  (3 shorter events, 0.0 us)
Async XLA Ops:
  0.0 1.2 %copy-start = (bf16[1,8,6,8192]{3,1,2,0:T(8,128)(2,1)S(1)}, bf16[1,8,6,8192]{3,1,2,0:T(8,128)(2,1)}, u32[]{:S(2)}) copy-start(bf16[1,8,6,8192]{3,1,2,0:T(8,128)(2,1)} %param.4) | copy-start | bytes 2359300
  0.0 0.7 %copy-start.1 = (s32[16]{0:T(128)S(1)}, s32[16]{0:T(128)}, u32[]{:S(2)}) copy-start(s32[16]{0:T(128)} %param.7) | copy-start | bytes 196
  0.0 0.7 %copy-start.2 = (s32[16,1]{0,1:T(1,128)S(1)}, s32[16,1]{0,1:T(1,128)}, u32[]{:S(2)}) copy-start(s32[16,1]{0,1:T(1,128)} %param.6) | copy-start | bytes 196
  0.0 0.8 %copy-start.3 = (s32[16]{0:T(128)S(1)}, s32[16]{0:T(128)}, u32[]{:S(2)}) copy-start(s32[16]{0:T(128)} %param.5) | copy-start | bytes 196

commit v4 on v3

--- a/solution.py
+++ b/solution.py
@@ -3,33 +3,34 @@
 
 import jax
 import jax.numpy as jnp
+import ml_dtypes
+import numpy as np
 from jax import lax
 from jax.experimental import pallas as pl
 from jax.experimental.pallas import tpu as pltpu
 from jax.sharding import PartitionSpec as P
 
 LAGS = 1024
-STEP = 64
 two_pi = 2.0 * math.pi
 MESH = pl.DeviceIdType.MESH
 
 
-def turn(first, step, num_bins):
+def lag_table(num_bins, chunk):
     period = 2 * num_bins
-    bins = first + step * lax.broadcasted_iota(jnp.int32, (8, LAGS), 0)
-    shift = lax.broadcasted_iota(jnp.int32, (8, LAGS), 1) - LAGS // 2
-    angle = (((bins * shift + num_bins) & (period - 1)) - num_bins).astype(jnp.float32) * (two_pi / period)
-    return jnp.cos(angle), jnp.sin(angle)
+    shift = np.arange(LAGS) - LAGS // 2
+    angles = np.mod(np.arange(num_bins)[:, None] * shift[None, :], period).astype(np.float32) * np.float32(two_pi / period)
+    both = np.stack([np.cos(angles), -np.sin(angles)]).reshape(2, num_bins // chunk, chunk, LAGS)
+    return both.transpose(1, 0, 2, 3).reshape(2 * num_bins, LAGS).astype(ml_dtypes.bfloat16)
 
 
 def kernel(
     n, groups, hours, pairs, chunk, chunks, helped, ahead, slack, scale,
-    spec_ref, pick_ref,
+    spec_ref, pick_ref, table_ref,
     out_ref,
-    gathered, picks, coarse_cos, coarse_sin, fine_cos, fine_sin, table, src, rcv, cross, acc, partial, landed, final,
+    gathered, picks, table, src, rcv, cross, acc, partial, landed, final,
     handed,
     send_sem, recv_sem, pick_send, pick_recv, give_send, give_recv, part_send, part_recv, fin_send, fin_recv,
-    hand_send, hand_recv,
+    hand_send, hand_recv, table_sem,
 ):
     z = lax.axis_index("sta")
     g = lax.axis_index("grp")
@@ -40,13 +41,19 @@
     pick_rows = pick_ref.shape[0]
     rows = 9 * pairs
     part = LAGS // hours
-    steps = chunk // STEP
     edge = (z == 0) | (z == n - 1)
     helper = (z == 1) | (z == n - 2)
     partner = jnp.where(z == 0, 1, jnp.where(z == 1, 0, jnp.where(z == n - 1, n - 2, n - 1)))
 
     for c in range(chunks):
         gathered[c, pl.ds(pl.multiple_of(z * block, 16), block), :] = spec_ref[:, c * chunk:(c + 1) * chunk]
+
+    def table_copy(c):
+        return pltpu.make_async_copy(
+            table_ref.at[pl.ds(pl.multiple_of((g * chunks + c) * (2 * chunk), 16), 2 * chunk)],
+            table.at[pl.ds(pl.multiple_of(c * (2 * chunk), 16), 2 * chunk)],
+            table_sem.at[c],
+        )
 
     barrier = pltpu.get_barrier_semaphore()
 
@@ -128,6 +135,10 @@
     def _(c):
         send_own(c)
 
+    @pl.loop(0, chunks)
+    def _(c):
+        table_copy(c).start()
+
     @pl.loop(1, groups)
     def _(d):
         pick_copy(d).start()
@@ -142,19 +153,6 @@
     picks[0, pl.ds(pl.multiple_of(g * pick_rows, 16), pick_rows), :] = pick_ref[...]
     acc[...] = jnp.zeros_like(acc)
 
-    num_bins = groups * chunks * chunk
-
-    def outer(cos_ref, sin_ref, count, first, step):
-        lc, ls = turn(0, step, num_bins)
-        hc, hs = turn(first, 8 * step, num_bins)
-        for i in range(count // 8):
-            a, b = hc[i:i + 1, :], hs[i:i + 1, :]
-            cos_ref[8 * i:8 * i + 8, :] = a * lc - b * ls
-            sin_ref[8 * i:8 * i + 8, :] = b * lc + a * ls
-
-    outer(fine_cos, fine_sin, STEP, 0, 1)
-    outer(coarse_cos, coarse_sin, chunks * steps, g * (chunks * chunk), STEP)
-
     def arrive(k, c):
         wanted = (c >= helped) | jnp.logical_not(edge)
 
@@ -173,19 +171,6 @@
             @pl.when(goes_left(c))
             def _():
                 line_copy(z + k, c, 1).start()
-
-    def make_table(c):
-        @pl.loop(0, steps)
-        def _(i):
-            row = c * steps + i
-            ca = coarse_cos[pl.ds(row, 1), :]
-            sa = coarse_sin[pl.ds(row, 1), :]
-            at = pl.multiple_of(c * (2 * chunk) + i * STEP, STEP)
-            for r in range(0, STEP, 16):
-                cb = fine_cos[r:r + 16, :]
-                sb = fine_sin[r:r + 16, :]
-                table[pl.ds(at + r, 16), :] = (ca * cb - sa * sb).astype(jnp.bfloat16)
-                table[pl.ds(at + chunk + r, 16), :] = -(sa * cb + ca * sb).astype(jnp.bfloat16)
 
     def compute(w, c):
         origin = jnp.where(w == 0, z, partner)
@@ -268,10 +253,6 @@
         def _():
             send_own(it + ahead)
 
-        @pl.when((it < chunks) & ((it >= helped) | jnp.logical_not(edge)))
-        def _():
-            make_table(it)
-
         @pl.loop(1, n)
         def _(k):
             c = it - slack * (k - 1)
@@ -294,6 +275,10 @@
                         give_copy(d).wait_recv()
 
         c = it - lag_steps
+        @pl.when((c >= 0) & (c < chunks))
+        def _():
+            table_copy(c).wait()
+
         turns = jnp.where(c >= helped, 1, jnp.where(edge, 0, jnp.where(helper, 2, 1)))
 
         @pl.loop(0, jnp.where((c >= 0) & (c < chunks), turns, 0))
@@ -399,17 +384,14 @@
     rows = 9 * pairs
     plane = groups * hours
     vmem = pl.BlockSpec(memory_space=pltpu.VMEM)
-    coarse = pltpu.VMEM((bins // STEP, LAGS), jnp.float32)
-    fine = pltpu.VMEM((STEP, LAGS), jnp.float32)
     out = pl.pallas_call(
         functools.partial(kernel, n, groups, hours, pairs, chunk, chunks, helped, 3, 2, scale),
         out_shape=jax.ShapeDtypeStruct((rows, LAGS), jnp.bfloat16),
-        in_specs=[vmem, vmem],
+        in_specs=[vmem, vmem, pl.BlockSpec(memory_space=pltpu.HBM)],
         out_specs=vmem,
         scratch_shapes=[
             pltpu.VMEM((chunks, n * block, chunk), jnp.bfloat16),
             pltpu.VMEM((held, groups * pick_rows, width), jnp.bfloat16),
-            coarse, coarse, fine, fine,
             pltpu.VMEM((2 * bins, LAGS), jnp.bfloat16),
             pltpu.VMEM((groups * pick_rows, chunk), jnp.float32),
             pltpu.VMEM((groups * pick_rows, chunk), jnp.float32),
@@ -431,6 +413,7 @@
             pltpu.SemaphoreType.DMA((hours,)),
             pltpu.SemaphoreType.DMA,
             pltpu.SemaphoreType.DMA,
+            pltpu.SemaphoreType.DMA((chunks,)),
         ],
         compiler_params=pltpu.CompilerParams(
             collective_id=0, has_side_effects=True, vmem_limit_bytes=48 * 1024 * 1024
@@ -438,7 +421,7 @@
         cost_estimate=pl.CostEstimate(
             flops=4 * groups * rows * bins * LAGS, bytes_accessed=4 * block * bins, transcendentals=0
         ),
-    )(spec, pick)
+    )(spec, pick, jnp.asarray(lag_table(num_bins, chunk)))
     return jnp.transpose(out.reshape(9, pairs, LAGS), (1, 0, 2)).astype(jnp.float32)
 
 

time: 55.1 us -> 53.9 us (0.978)
  Pallas kernels: 52.8 us -> 51.6 us
  other arithmetic: 1.06 us -> 1.82 us
  local copies, waits for them, and re-layouts: 1 us -> 0.26 us
    pallas_call x1, Pallas kernels: 52.8 us -> 51.6 us  [body(): pl.pallas_call(functools.partial(kernel, n, groups, hours, pairs, chunk,...]
    add x1, other arithmetic: 0.01 us -> 0.76 us  [body(): pair_owner[:, 0] * block + pair_row]
    unnamed x8 -> x2, local copies, waits for them, and re-layouts: 0.81 us -> 0.08 us
where the time goes in v4:
time: 53.9 us; the launch traced here: 53.7 us
  Pallas kernels  51.6 us (96%)
  other arithmetic  1.82 us (3%)
    pallas_call x1, Pallas kernels, body(): pl.pallas_call(functools.partial(kernel, n, groups, hours, pairs, chunk,...  51.6 us

profile of v4, /device:TPU:1, one launch (start us, length us, event | category | flops | bytes accessed | tf_op | source)
XLA Modules:
  0.0 53.7 jit_solution(6814991461873793277)
XLA Ops:
  0.0 0.0 copy-start
  0.0 0.8 %bitcast_add_fusion = (s32[16]{0:T(128)S(1)}, s32[16]{0:T(128)S(1)}) fusion(s32[16]{0:T(128)} %param.8, s32[16,1]{0,1:T(1,128)} %param.7, s32[16]{0:T(128)} %param.6), kind=kLoop, calls=%fused_computation.8 | loop fusion | flops 48 | bytes 320 | tf_op jit(solution)/shard_map/add | solution.py:378
  0.8 0.1 broadcast_add_fusion.1
  0.8 0.1 add.54
  0.9 0.1 add.58
  1.0 0.1 fusion.1.pick_ref
  1.1 0.1 copy-done
  1.2 51.6 %shard_map.55 = bf16[144,1024]{1,0:T(8,128)(2,1)S(1)} custom-call(bf16[48,4096]{1,0:T(8,128)(2,1)S(1)} %dynamic-slice_bitcast_fusion.spec_ref, bf16[96,256]{1,0:T(8,128)(2,1)S(1)} %fusion.1.pick_ref, bf16[16384,1024]{1,0:T(8,128)(2,1)} %constant.21.clone.table_ref), custom_call_target="tpu_custom_call" | custom-call | flops 4831838208 | bytes 786432 | tf_op jit(solution)/shard_map/pallas_call | solution.py:387
  52.9 0.9 %convert_bitcast_fusion = f32[16,9,1024]{2,0,1:T(8,128)} fusion(bf16[9,16,1024]{2,1,0:T(8,128)(2,1)S(1)} %bitcast.12), kind=kLoop, calls=%fused_computation | loop fusion | flops 147456 | bytes 884736 | tf_op jit(solution)/shard_map/convert_element_type | solution.py:425
  (2 shorter events, 0.0 us)
Async XLA Ops:
  0.0 1.2 %copy-start = (bf16[1,8,6,8192]{3,1,2,0:T(8,128)(2,1)S(1)}, bf16[1,8,6,8192]{3,1,2,0:T(8,128)(2,1)}, u32[]{:S(2)}) copy-start(bf16[1,8,6,8192]{3,1,2,0:T(8,128)(2,1)} %param.5) | copy-start | bytes 2359300

commit v5 on v4

--- a/solution.py
+++ b/solution.py
@@ -27,9 +27,9 @@
     n, groups, hours, pairs, chunk, chunks, helped, ahead, slack, scale,
     spec_ref, pick_ref, table_ref,
     out_ref,
-    gathered, picks, table, src, rcv, cross, acc, partial, landed, final,
+    gathered, picks, table, src, rcv, cross, acc, partial, paired, mid, landed, final,
     handed,
-    send_sem, recv_sem, pick_send, pick_recv, give_send, give_recv, part_send, part_recv, fin_send, fin_recv,
+    send_sem, recv_sem, pick_send, pick_recv, give_send, give_recv, pair_send, pair_recv, part_send, part_recv, fin_send, fin_recv,
     hand_send, hand_recv, table_sem,
 ):
     z = lax.axis_index("sta")
@@ -203,34 +203,57 @@
             preferred_element_type=jnp.float32,
         )
 
-    lags = pl.ds(pl.multiple_of(h * part, 128), part)
+    quads = hours // 2
+    q, odd = h // 2, lax.rem(h, 2)
+    half = quads * part
+    my_half = pl.ds(pl.multiple_of(odd * half, 128), half)
+    other_half = pl.ds(pl.multiple_of((1 - odd) * half, 128), half)
+    in_half = pl.ds(pl.multiple_of(q * part, 128), part)
+    lag_start = odd * half + q * part
+    lags = pl.ds(pl.multiple_of(lag_start, 128), part)
     own_rows = pl.ds(pl.multiple_of(g * rows, 16), rows)
+    owners = groups * quads
+
+    def pair_copy(w):
+        return pltpu.make_async_remote_copy(
+            src_ref=partial.at[w],
+            dst_ref=paired.at[w],
+            send_sem=pair_send.at[w],
+            recv_sem=pair_recv.at[w],
+            device_id={"hr": 2 * q + (1 - odd)},
+            device_id_type=MESH,
+        )
 
     def part_copy(w, d):
-        t = lax.rem(me + d, plane)
-        tg, th = t // hours, lax.rem(t, hours)
-        return pltpu.make_async_remote_copy(
-            src_ref=partial.at[
-                w, pl.ds(pl.multiple_of(tg * rows, 16), rows), pl.ds(pl.multiple_of(th * part, 128), part)
+        t = lax.rem(g * quads + q + d, owners)
+        tg, tq = t // quads, lax.rem(t, quads)
+        return pltpu.make_async_remote_copy(
+            src_ref=mid.at[
+                w, pl.ds(pl.multiple_of(tg * rows, 16), rows), pl.ds(pl.multiple_of(tq * part, 128), part)
             ],
             dst_ref=landed.at[w, d],
             send_sem=part_send.at[w, d],
             recv_sem=part_recv.at[w, d],
-            device_id={"grp": tg, "hr": th},
-            device_id_type=MESH,
-        )
+            device_id={"grp": tg, "hr": 2 * tq + odd},
+            device_id_type=MESH,
+        )
+
+    def pair_up(w):
+        partial[w] = acc[w, :, other_half].astype(jnp.bfloat16)
+        pair_copy(w).start()
 
     def scatter(w):
-        partial[w] = acc[w].astype(jnp.bfloat16)
-
-        @pl.loop(1, plane)
+        pair_copy(w).wait_recv()
+        mid[w] = (acc[w, :, my_half] + paired[w].astype(jnp.float32)).astype(jnp.bfloat16)
+
+        @pl.loop(1, owners)
         def _(d):
             part_copy(w, d).start()
 
     def collect(w):
-        final[...] = acc[w, own_rows, lags]
-
-        @pl.loop(1, plane)
+        final[...] = acc[w, own_rows, lags] + paired[w, own_rows, in_half].astype(jnp.float32)
+
+        @pl.loop(1, owners)
         def _(d):
             part_copy(w, d).wait_recv()
             final[...] += landed[w, d].astype(jnp.float32)
@@ -288,13 +311,19 @@
         if helped:
             @pl.when(helper & (c == helped - 1))
             def _():
+                pair_up(1)
+
+            @pl.when(helper & (c == helped))
+            def _():
                 scatter(1)
 
-            @pl.when(helper & (c == helped + 1))
-            def _():
-                collect(1)
-                handed[...] = final[...].astype(jnp.bfloat16)
-                hand_copy().start()
+    pair_up(0)
+    if helped:
+        @pl.when(helper)
+        def _():
+            collect(1)
+            handed[...] = final[...].astype(jnp.bfloat16)
+            hand_copy().start()
 
     scatter(0)
     collect(0)
@@ -304,7 +333,7 @@
             hand_copy().wait_recv()
             final[...] += landed[0, 0].astype(jnp.float32)
 
-    lag = (h * part + lax.broadcasted_iota(jnp.int32, (8, part), 1)).astype(jnp.float32)
+    lag = (lag_start + lax.broadcasted_iota(jnp.int32, (8, part), 1)).astype(jnp.float32)
     taper = (0.75 - 0.25 * jnp.cos(two_pi * (lag + 0.5) / LAGS)) * scale
     out_ref[:, lags] = (final[...] * taper[0:1, :]).astype(jnp.bfloat16)
 
@@ -322,7 +351,9 @@
     def _(d):
         fin_copy(d).start()
 
-    @pl.loop(1, plane)
+    pair_copy(0).wait_send()
+
+    @pl.loop(1, owners)
     def _(d):
         part_copy(0, d).wait_send()
 
@@ -330,8 +361,9 @@
         @pl.when(helper)
         def _():
             hand_copy().wait_send()
-
-            @pl.loop(1, plane)
+            pair_copy(1).wait_send()
+
+            @pl.loop(1, owners)
             def _(d):
                 part_copy(1, d).wait_send()
 
@@ -382,7 +414,6 @@
 
     scale = 1.0 / (hours * spectra.shape[0] * math.sqrt(num_bins))
     rows = 9 * pairs
-    plane = groups * hours
     vmem = pl.BlockSpec(memory_space=pltpu.VMEM)
     out = pl.pallas_call(
         functools.partial(kernel, n, groups, hours, pairs, chunk, chunks, helped, 3, 2, scale),
@@ -397,8 +428,10 @@
             pltpu.VMEM((groups * pick_rows, chunk), jnp.float32),
             pltpu.VMEM((groups * rows, 2 * chunk), jnp.bfloat16),
             pltpu.VMEM((held, groups * rows, LAGS), jnp.float32),
-            pltpu.VMEM((held, groups * rows, LAGS), jnp.bfloat16),
-            pltpu.VMEM((held, plane, rows, LAGS // hours), jnp.bfloat16),
+            pltpu.VMEM((held, groups * rows, LAGS // 2), jnp.bfloat16),
+            pltpu.VMEM((held, groups * rows, LAGS // 2), jnp.bfloat16),
+            pltpu.VMEM((held, groups * rows, LAGS // 2), jnp.bfloat16),
+            pltpu.VMEM((held, groups * hours // 2, rows, LAGS // hours), jnp.bfloat16),
             pltpu.VMEM((rows, LAGS // hours), jnp.float32),
             pltpu.VMEM((rows, LAGS // hours), jnp.bfloat16),
             pltpu.SemaphoreType.DMA((2, n, chunks)),
@@ -407,8 +440,10 @@
             pltpu.SemaphoreType.DMA((groups,)),
             pltpu.SemaphoreType.DMA((groups,)),
             pltpu.SemaphoreType.DMA((groups,)),
-            pltpu.SemaphoreType.DMA((held, plane)),
-            pltpu.SemaphoreType.DMA((held, plane)),
+            pltpu.SemaphoreType.DMA((held,)),
+            pltpu.SemaphoreType.DMA((held,)),
+            pltpu.SemaphoreType.DMA((held, groups * hours // 2)),
+            pltpu.SemaphoreType.DMA((held, groups * hours // 2)),
             pltpu.SemaphoreType.DMA((hours,)),
             pltpu.SemaphoreType.DMA((hours,)),
             pltpu.SemaphoreType.DMA,

time: 53.9 us -> 47.6 us (0.88)
  Pallas kernels: 51.6 us -> 45.3 us
    pallas_call x1, Pallas kernels: 51.6 us -> 45.3 us  [body(): pl.pallas_call(functools.partial(kernel, n, groups, hours, pairs, chunk,...]
where the time goes in v5:
time: 47.6 us; the launch traced here: 47.4 us
  Pallas kernels  45.3 us (95%)
  other arithmetic  1.82 us (4%)
    pallas_call x1, Pallas kernels, body(): pl.pallas_call(functools.partial(kernel, n, groups, hours, pairs, chunk,...  45.3 us

profile of v5, /device:TPU:1, one launch (start us, length us, event | category | flops | bytes accessed | tf_op | source)
XLA Modules:
  0.0 47.4 jit_solution(15462401045040388295)
XLA Ops:
  0.0 0.0 copy-start
  0.0 0.8 %bitcast_add_fusion = (s32[16]{0:T(128)S(1)}, s32[16]{0:T(128)S(1)}) fusion(s32[16]{0:T(128)} %param.8, s32[16,1]{0,1:T(1,128)} %param.7, s32[16]{0:T(128)} %param.6), kind=kLoop, calls=%fused_computation.8 | loop fusion | flops 48 | bytes 320 | tf_op jit(solution)/shard_map/add | solution.py:410
  0.8 0.1 broadcast_add_fusion.1
  0.8 0.1 add.54
  0.9 0.1 add.58
  1.0 0.1 fusion.1.pick_ref
  1.1 0.1 copy-done
  1.2 45.3 %shard_map.55 = bf16[144,1024]{1,0:T(8,128)(2,1)S(1)} custom-call(bf16[48,4096]{1,0:T(8,128)(2,1)S(1)} %dynamic-slice_bitcast_fusion.spec_ref, bf16[96,256]{1,0:T(8,128)(2,1)S(1)} %fusion.1.pick_ref, bf16[16384,1024]{1,0:T(8,128)(2,1)} %constant.21.clone.table_ref), custom_call_target="tpu_custom_call" | custom-call | flops 4831838208 | bytes 786432 | tf_op jit(solution)/shard_map/pallas_call | solution.py:418
  46.6 0.9 %convert_bitcast_fusion = f32[16,9,1024]{2,0,1:T(8,128)} fusion(bf16[9,16,1024]{2,1,0:T(8,128)(2,1)S(1)} %bitcast.12), kind=kLoop, calls=%fused_computation | loop fusion | flops 147456 | bytes 884736 | tf_op jit(solution)/shard_map/convert_element_type | solution.py:460
  (2 shorter events, 0.0 us)
Async XLA Ops:
  0.0 1.2 %copy-start = (bf16[1,8,6,8192]{3,1,2,0:T(8,128)(2,1)S(1)}, bf16[1,8,6,8192]{3,1,2,0:T(8,128)(2,1)}, u32[]{:S(2)}) copy-start(bf16[1,8,6,8192]{3,1,2,0:T(8,128)(2,1)} %param.5) | copy-start | bytes 2359300

commit v6 on v5

--- a/solution.py
+++ b/solution.py
@@ -394,9 +394,9 @@
     _, sta_dev, comps, num_bins = spectra.shape
     pairs = pair_source.shape[0]
     bins = num_bins // groups
-    chunk = min(512, bins)
+    chunk = min(256, bins)
     chunks = bins // chunk
-    helped = 3 * chunks // 8 if n >= 4 else 0
+    helped = 5 * chunks // 16 if n >= 4 else 0
     held = 2 if helped else 1
     block = comps * sta_dev
     pick_rows = comps * pairs
@@ -416,7 +416,7 @@
     rows = 9 * pairs
     vmem = pl.BlockSpec(memory_space=pltpu.VMEM)
     out = pl.pallas_call(
-        functools.partial(kernel, n, groups, hours, pairs, chunk, chunks, helped, 3, 2, scale),
+        functools.partial(kernel, n, groups, hours, pairs, chunk, chunks, helped, 6, 2, scale),
         out_shape=jax.ShapeDtypeStruct((rows, LAGS), jnp.bfloat16),
         in_specs=[vmem, vmem, pl.BlockSpec(memory_space=pltpu.HBM)],
         out_specs=vmem,

time: 47.6 us -> 54.4 us (1.14)
  Pallas kernels: 45.3 us -> 52.1 us
    pallas_call x1, Pallas kernels: 45.3 us -> 52.1 us  [body(): pl.pallas_call(functools.partial(kernel, n, groups, hours, pairs, chunk,...]
where the time goes in v6:
time: 54.4 us; the launch traced here: 54.2 us
  Pallas kernels  52.1 us (96%)
  other arithmetic  1.82 us (3%)
    pallas_call x1, Pallas kernels, body(): pl.pallas_call(functools.partial(kernel, n, groups, hours, pairs, chunk,...  52.1 us

profile of v6, /device:TPU:1, one launch (start us, length us, event | category | flops | bytes accessed | tf_op | source)
XLA Modules:
  0.0 54.2 jit_solution(10214587064938223557)
XLA Ops:
  0.0 0.0 copy-start
  0.0 0.8 %bitcast_add_fusion = (s32[16]{0:T(128)S(1)}, s32[16]{0:T(128)S(1)}) fusion(s32[16]{0:T(128)} %param.8, s32[16,1]{0,1:T(1,128)} %param.7, s32[16]{0:T(128)} %param.6), kind=kLoop, calls=%fused_computation.8 | loop fusion | flops 48 | bytes 320 | tf_op jit(solution)/shard_map/add | solution.py:410
  0.8 0.1 broadcast_add_fusion.1
  0.8 0.1 add.54
  0.9 0.1 add.58
  1.0 0.1 fusion.1.pick_ref
  1.1 0.1 copy-done
  1.2 52.1 %shard_map.55 = bf16[144,1024]{1,0:T(8,128)(2,1)S(1)} custom-call(bf16[48,4096]{1,0:T(8,128)(2,1)S(1)} %dynamic-slice_bitcast_fusion.spec_ref, bf16[96,256]{1,0:T(8,128)(2,1)S(1)} %fusion.1.pick_ref, bf16[16384,1024]{1,0:T(8,128)(2,1)} %constant.21.clone.table_ref), custom_call_target="tpu_custom_call" | custom-call | flops 4831838208 | bytes 786432 | tf_op jit(solution)/shard_map/pallas_call | solution.py:418
  53.3 0.9 %convert_bitcast_fusion = f32[16,9,1024]{2,0,1:T(8,128)} fusion(bf16[9,16,1024]{2,1,0:T(8,128)(2,1)S(1)} %bitcast.12), kind=kLoop, calls=%fused_computation | loop fusion | flops 147456 | bytes 884736 | tf_op jit(solution)/shard_map/convert_element_type | solution.py:460
  (2 shorter events, 0.0 us)
Async XLA Ops:
  0.0 1.2 %copy-start = (bf16[1,8,6,8192]{3,1,2,0:T(8,128)(2,1)S(1)}, bf16[1,8,6,8192]{3,1,2,0:T(8,128)(2,1)}, u32[]{:S(2)}) copy-start(bf16[1,8,6,8192]{3,1,2,0:T(8,128)(2,1)} %param.5) | copy-start | bytes 2359300

commit v7 on v5

--- a/solution.py
+++ b/solution.py
@@ -131,7 +131,9 @@
             device_id_type=MESH,
         )
 
-    @pl.loop(0, min(ahead, chunks))
+    at_once = jnp.where(edge, chunks, min(ahead, chunks))
+
+    @pl.loop(0, at_once)
     def _(c):
         send_own(c)
 
@@ -272,12 +274,13 @@
 
     @pl.loop(0, chunks + slack * max(n - 2, 0))
     def _(it):
-        @pl.when(it + ahead < chunks)
+        @pl.when((it + ahead < chunks) & jnp.logical_not(edge))
         def _():
             send_own(it + ahead)
 
         @pl.loop(1, n)
-        def _(k):
+        def _(back):
+            k = n - back
             c = it - slack * (k - 1)
 
             @pl.when((c >= 0) & (c < chunks))
@@ -396,7 +399,7 @@
     bins = num_bins // groups
     chunk = min(512, bins)
     chunks = bins // chunk
-    helped = 3 * chunks // 8 if n >= 4 else 0
+    helped = 5 * chunks // 16 if n >= 4 else 0
     held = 2 if helped else 1
     block = comps * sta_dev
     pick_rows = comps * pairs

time: 47.6 us -> 52.5 us (1.10)
  Pallas kernels: 45.3 us -> 50.3 us
    pallas_call x1, Pallas kernels: 45.3 us -> 50.3 us  [body(): pl.pallas_call(functools.partial(kernel, n, groups, hours, pairs, chunk,...]
where the time goes in v7:
time: 52.5 us; the launch traced here: 52.4 us
  Pallas kernels  50.3 us (96%)
  other arithmetic  1.82 us (3%)
    pallas_call x1, Pallas kernels, body(): pl.pallas_call(functools.partial(kernel, n, groups, hours, pairs, chunk,...  50.3 us

profile of v7, /device:TPU:1, one launch (start us, length us, event | category | flops | bytes accessed | tf_op | source)
XLA Modules:
  0.0 52.4 jit_solution(1099475994252327783)
XLA Ops:
  0.0 0.0 copy-start
  0.0 0.8 %bitcast_add_fusion = (s32[16]{0:T(128)S(1)}, s32[16]{0:T(128)S(1)}) fusion(s32[16]{0:T(128)} %param.8, s32[16,1]{0,1:T(1,128)} %param.7, s32[16]{0:T(128)} %param.6), kind=kLoop, calls=%fused_computation.8 | loop fusion | flops 48 | bytes 320 | tf_op jit(solution)/shard_map/add | solution.py:413
  0.8 0.1 broadcast_add_fusion.1
  0.8 0.1 add.54
  0.9 0.1 add.58
  1.0 0.1 fusion.1.pick_ref
  1.1 0.1 copy-done
  1.2 50.3 %shard_map.55 = bf16[144,1024]{1,0:T(8,128)(2,1)S(1)} custom-call(bf16[48,4096]{1,0:T(8,128)(2,1)S(1)} %dynamic-slice_bitcast_fusion.spec_ref, bf16[96,256]{1,0:T(8,128)(2,1)S(1)} %fusion.1.pick_ref, bf16[16384,1024]{1,0:T(8,128)(2,1)} %constant.21.clone.table_ref), custom_call_target="tpu_custom_call" | custom-call | flops 4831838208 | bytes 786432 | tf_op jit(solution)/shard_map/pallas_call | solution.py:421
  51.5 0.9 %convert_bitcast_fusion = f32[16,9,1024]{2,0,1:T(8,128)} fusion(bf16[9,16,1024]{2,1,0:T(8,128)(2,1)S(1)} %bitcast.12), kind=kLoop, calls=%fused_computation | loop fusion | flops 147456 | bytes 884736 | tf_op jit(solution)/shard_map/convert_element_type | solution.py:463
  (2 shorter events, 0.0 us)
Async XLA Ops:
  0.0 1.2 %copy-start = (bf16[1,8,6,8192]{3,1,2,0:T(8,128)(2,1)S(1)}, bf16[1,8,6,8192]{3,1,2,0:T(8,128)(2,1)}, u32[]{:S(2)}) copy-start(bf16[1,8,6,8192]{3,1,2,0:T(8,128)(2,1)} %param.5) | copy-start | bytes 2359300

commit v8 on v5

--- a/solution.py
+++ b/solution.py
@@ -396,7 +396,7 @@
     bins = num_bins // groups
     chunk = min(512, bins)
     chunks = bins // chunk
-    helped = 3 * chunks // 8 if n >= 4 else 0
+    helped = chunks // 2 if n >= 4 else 0
     held = 2 if helped else 1
     block = comps * sta_dev
     pick_rows = comps * pairs

time: 47.6 us -> 48.1 us (1.011)
  Pallas kernels: 45.3 us -> 45.9 us
    pallas_call x1, Pallas kernels: 45.3 us -> 45.9 us  [body(): pl.pallas_call(functools.partial(kernel, n, groups, hours, pairs, chunk,...]
where the time goes in v8:
time: 48.1 us; the launch traced here: 48 us
  Pallas kernels  45.9 us (95%)
  other arithmetic  1.82 us (4%)
    pallas_call x1, Pallas kernels, body(): pl.pallas_call(functools.partial(kernel, n, groups, hours, pairs, chunk,...  45.9 us

profile of v8, /device:TPU:1, one launch (start us, length us, event | category | flops | bytes accessed | tf_op | source)
XLA Modules:
  0.0 48.0 jit_solution(5141820345486334440)
XLA Ops:
  0.0 0.0 copy-start
  0.0 0.8 %bitcast_add_fusion = (s32[16]{0:T(128)S(1)}, s32[16]{0:T(128)S(1)}) fusion(s32[16]{0:T(128)} %param.8, s32[16,1]{0,1:T(1,128)} %param.7, s32[16]{0:T(128)} %param.6), kind=kLoop, calls=%fused_computation.8 | loop fusion | flops 48 | bytes 320 | tf_op jit(solution)/shard_map/add | solution.py:410
  0.8 0.1 broadcast_add_fusion.1
  0.8 0.1 add.54
  0.9 0.1 add.58
  1.0 0.1 fusion.1.pick_ref
  1.1 0.1 copy-done
  1.2 45.9 %shard_map.55 = bf16[144,1024]{1,0:T(8,128)(2,1)S(1)} custom-call(bf16[48,4096]{1,0:T(8,128)(2,1)S(1)} %dynamic-slice_bitcast_fusion.spec_ref, bf16[96,256]{1,0:T(8,128)(2,1)S(1)} %fusion.1.pick_ref, bf16[16384,1024]{1,0:T(8,128)(2,1)} %constant.21.clone.table_ref), custom_call_target="tpu_custom_call" | custom-call | flops 4831838208 | bytes 786432 | tf_op jit(solution)/shard_map/pallas_call | solution.py:418
  47.1 0.9 %convert_bitcast_fusion = f32[16,9,1024]{2,0,1:T(8,128)} fusion(bf16[9,16,1024]{2,1,0:T(8,128)(2,1)S(1)} %bitcast.12), kind=kLoop, calls=%fused_computation | loop fusion | flops 147456 | bytes 884736 | tf_op jit(solution)/shard_map/convert_element_type | solution.py:460
  (2 shorter events, 0.0 us)
Async XLA Ops:
  0.0 1.2 %copy-start = (bf16[1,8,6,8192]{3,1,2,0:T(8,128)(2,1)S(1)}, bf16[1,8,6,8192]{3,1,2,0:T(8,128)(2,1)}, u32[]{:S(2)}) copy-start(bf16[1,8,6,8192]{3,1,2,0:T(8,128)(2,1)} %param.5) | copy-start | bytes 2359300
